TPU v7x, 128 devices: a whole 4x4x4 slice. The times are simulated.
128 devices in a mesh: row: 16 (over x_lo, y, core), col: 8 (over z, x_hi).
Axes of the slice: x: 4 (x_hi: 2, x_lo: 2; x = x_hi * 2 + x_lo), y: 4, z: 4, core: 2. Of those that a mesh axis runs over, the one named last changes fastest.
Arguments:
- left_proj: bfloat16 [1024, 4096], P(('row', 'col')), may hold values from -6 to 6
- right_proj: bfloat16 [1024, 4096], P(('col', 'row')), may hold values from -6 to 6
- out_weight: bfloat16 [1024, 128], replicated, may hold values from -0.1875 to 0.1875
- out_bias: float32 [128], replicated, may hold values from -3 to 3
- pair_cotangent: bfloat16 [1024, 1024, 128], P('row', 'col'), may hold values from -6 to 6
Outputs:
- pair_update: bfloat16 [1024, 1024, 128], P('row', 'col')
- grad_left: float32 [1024, 4096], P(('row', 'col'))
- grad_right: float32 [1024, 4096], P(('col', 'row'))
- grad_weight: float32 [1024, 128], replicated
- grad_bias: float32 [128], replicated
All inputs are finite; a program needn't handle non-finite values.
Results may differ from a plain program's by a relative error of at most 0.0031.
Values may be sent and summed in bfloat16 or wider, within the bound.
A program may use at most 128 MiB of HBM per device.

v0:
```python
import jax
import jax.numpy as jnp
from jax import lax
from jax.sharding import PartitionSpec as P

C = 32
CZ = 128
S = 128


def per_device(left_proj, right_proj, out_weight, out_bias, pair_cotangent):
    inv = 1.0 / S
    left = lax.all_gather(left_proj, "col", axis=0, tiled=True)
    right = lax.all_gather(right_proj, "row", axis=0, tiled=True)
    rows_i = left.shape[0]
    rows_j = right.shape[0]
    left3 = left.reshape(rows_i, S, C)
    right3 = right.reshape(rows_j, S, C)
    w_t = out_weight.T
    blocks = rows_i // 8
    left_blocks = left3.reshape(blocks, 8, S, C)
    cot_blocks = pair_cotangent.reshape(blocks, 8, rows_j, CZ)

    def block(carry, xs):
        grad_w, grad_b, grad_r = carry
        left_blk, cot_blk = xs
        outer = (
            jnp.einsum("isa,jsb->ijab", left_blk, right3, preferred_element_type=jnp.float32) * inv
        ).astype(jnp.bfloat16)
        flat = outer.reshape(8 * rows_j, C * C)
        pair = (jnp.dot(flat, out_weight, preferred_element_type=jnp.float32) + out_bias).astype(
            jnp.bfloat16
        )
        cot_flat = cot_blk.reshape(8 * rows_j, CZ)
        grad_w = grad_w + lax.dot_general(
            flat, cot_flat, (((0,), (0,)), ((), ())), preferred_element_type=jnp.float32
        )
        grad_b = grad_b + jnp.sum(cot_flat.astype(jnp.float32), axis=0)
        d_outer = jnp.dot(cot_flat, w_t, preferred_element_type=jnp.float32).astype(jnp.bfloat16)
        d_four = d_outer.reshape(8, rows_j, C, C)
        grad_r = (
            grad_r
            + jnp.einsum("ijab,isa->jsb", d_four, left_blk, preferred_element_type=jnp.float32)
            * inv
        )
        grad_l = (
            jnp.einsum("ijab,jsb->isa", d_four, right3, preferred_element_type=jnp.float32) * inv
        )
        return ((grad_w, grad_b, grad_r), (pair.reshape(8, rows_j, CZ), grad_l.reshape(8, S * C)))

    init = (
        jnp.zeros((C * C, CZ), jnp.float32),
        jnp.zeros((CZ,), jnp.float32),
        jnp.zeros((rows_j, S, C), jnp.float32),
    )
    (grad_w, grad_b, grad_r), (pairs, grads_l) = lax.scan(block, init, (left_blocks, cot_blocks))
    pair_update = pairs.reshape(rows_i, rows_j, CZ)
    grad_left = lax.psum_scatter(
        grads_l.reshape(rows_i, S * C), "col", scatter_dimension=0, tiled=True
    )
    grad_right = lax.psum_scatter(
        grad_r.reshape(rows_j, S * C), "row", scatter_dimension=0, tiled=True
    )
    grad_weight, grad_bias = lax.psum((grad_w, grad_b), ("row", "col"))
    return (pair_update, grad_left, grad_right, grad_weight, grad_bias)


def solution(mesh):
    return jax.shard_map(
        per_device,
        mesh=mesh,
        in_specs=(
            P(("row", "col"), None),
            P(("col", "row"), None),
            P(),
            P(),
            P("row", "col", None),
        ),
        out_specs=(
            P("row", "col", None),
            P(("row", "col"), None),
            P(("col", "row"), None),
            P(),
            P(),
        ),
        check_vma=False,
    )
```

profile of v0, /device:TPU:1, one launch (start us, length us, event | category | flops | bytes accessed | tf_op | source)
XLA Modules:
  0.0 501.1 jit_solution(9906001449048993820)
XLA Ops:
  9.1 33.5 %all_gather.6 = bf16[64,4096]{1,0:T(8,128)(2,1)S(1)} all-gather(bf16[8,4096]{1,0:T(8,128)(2,1)} %param.7), channel_id=1, replica_groups=mesh['row'=16,'col'=8] {'col'}, dimensions={0}, use_global_device_ids=true | all-gather | bytes 589824 | tf_op jit(solution)/shard_map/all_gather | solution.py:13
  42.6 1.6 reshape_reshape.3
  44.2 1.5 copy.31
  46.1 1.6 copy.29
  48.7 156.4 %while.19 = (s32[]{:T(128)}, f32[1024,128]{1,0:T(8,128)}, f32[128]{0:T(128)S(1)}, f32[128,128,32]{0,1,2:T(8,128)}, bf16[8,8,128,128]{3,2,1,0:T(8,128)(2,1)}, /*i...) while((s32[]{:T(128)}, f32[1024,128]{1,0:T(8,128)}, ...), condition=%wide.region_2.3_spmd.clone, body=%wide.region_0.2_spmd.clone.sunk | while | flops 1616150656 | bytes 60033904 | solution.py:56
  50.0 2.0 convolution_convert_fusion.2
  52.0 2.9 copy.71
  57.0 2.6 bitcast_add_fusion.2
  59.7 1.2 copy.73
  60.9 1.3 broadcast_in_dim.32
  62.9 1.5 fusion.65
  64.4 1.4 copy.70
  69.5 2.0 convolution_convert_fusion.2
  71.5 2.9 copy.71
  76.6 2.6 bitcast_add_fusion.2
  79.2 1.2 copy.73
  80.5 1.3 broadcast_in_dim.32
  82.4 1.5 fusion.65
  84.0 1.4 copy.70
  89.0 2.0 convolution_convert_fusion.2
  91.0 2.9 copy.71
  96.1 2.6 bitcast_add_fusion.2
  100.0 1.3 broadcast_in_dim.32
  102.0 1.5 fusion.65
  103.6 1.4 copy.70
  108.6 2.0 convolution_convert_fusion.2
  110.6 2.9 copy.71
  115.7 2.6 bitcast_add_fusion.2
  118.3 1.2 copy.73
  119.6 1.3 broadcast_in_dim.32
  121.5 1.5 fusion.65
  123.1 1.4 copy.70
  128.2 2.0 convolution_convert_fusion.2
  130.2 2.9 copy.71
  135.2 2.6 bitcast_add_fusion.2
  139.1 1.3 broadcast_in_dim.32
  141.1 1.5 fusion.65
  142.7 1.4 copy.70
  147.7 2.0 convolution_convert_fusion.2
  149.7 2.9 copy.71
  154.8 2.6 bitcast_add_fusion.2
  157.5 1.2 copy.73
  158.7 1.3 broadcast_in_dim.32
  160.6 1.5 fusion.65
  162.2 1.4 copy.70
  167.3 2.0 convolution_convert_fusion.2
  169.3 2.9 copy.71
  174.3 2.6 bitcast_add_fusion.2
  178.3 1.3 broadcast_in_dim.32
  180.2 1.5 fusion.65
  181.8 1.4 copy.70
  186.8 2.0 convolution_convert_fusion.2
  188.8 2.9 copy.71
  193.9 2.6 bitcast_add_fusion.2
  197.8 1.3 broadcast_in_dim.32
  199.7 1.5 fusion.65
  201.3 1.4 copy.70
  206.1 2.8 copy.33
  208.9 1.9 copy.38
  210.8 70.3 %psum.15 = f32[128]{0:T(128)} all-reduce(f32[128]{0:T(128)S(1)} %get-tuple-element.75), channel_id=1, replica_groups=mesh['row'=16,'col'=8] {'row','col'}, use_global_device_ids=true, to_apply=%region_6.7 | all-reduce | flops 128 | bytes 1024 | tf_op jit(solution)/shard_map/psum | solution.py:64
  281.1 75.1 %all-reduce.2.cloned.1.call-done = f32[1024,128]{1,0:T(8,128)} async-done(((f32[1024,128]{1,0:T(8,128)}), f32[1024,128]{1,0:T(8,128)}) %all-reduce.2.cloned.1.call-update) | async-done | bytes 524304 | tf_op jit(solution)/shard_map/psum | solution.py:64
  356.2 73.1 %reduce-scatter.5.cloned.1.call-done = f32[8,4096]{1,0:T(8,128)} async-done(((f32[64,4096]{1,0:T(8,128)}), f32[8,4096]{1,0:T(8,128)}) %reduce-scatter.5.cloned.1.call-update) | async-done | bytes 131088 | tf_op jit(solution)/shard_map/reduce_scatter | solution.py:58
  429.3 63.3 %reduce-scatter.7.cloned.1.call-done = f32[8,4096]{1,0:T(8,128)} async-done(((f32[128,4096]{1,0:T(8,128)}), f32[8,4096]{1,0:T(8,128)}) %reduce-scatter.7.cloned.1.call-update) | async-done | bytes 131088
  492.7 1.9 copy.95
  (198 shorter events, 61.4 us)
Async XLA Ops:
  7.2 38.9 %all-gather.2.cloned.1.call-start = ((), (), s32[]{:S(2)}) async-start(), calls=%async_computation.2 | async-start | bytes 1114112 | tf_op jit(solution)/shard_map/all_gather | solution.py:14
  7.9 348.3 %all-reduce.2.cloned.1.call-start = ((), (), s32[]{:S(2)}) async-start(), calls=%async_computation.4 | async-start | bytes 1048576 | tf_op jit(solution)/shard_map/psum | solution.py:64
  45.7 3.0 copy-start.7
  48.7 1.2 copy-start.2
  55.4 1.6 copy-start
  59.7 4.7 copy-start.1
  64.4 1.4 copy-start.4
  65.8 1.0 copy-start.6
  66.8 0.8 copy-start.5
  66.8 1.5 copy-start.3
  68.3 1.2 copy-start.2
  75.0 1.6 copy-start
  79.2 4.8 copy-start.1
  84.0 1.4 copy-start.4
  85.4 1.0 copy-start.6
  86.3 0.8 copy-start.5
  86.3 1.5 copy-start.3
  87.8 1.2 copy-start.2
  94.5 1.6 copy-start
  98.8 4.8 copy-start.1
  103.5 1.4 copy-start.4
  104.9 1.0 copy-start.6
  105.9 0.8 copy-start.5
  105.9 1.5 copy-start.3
  107.4 1.2 copy-start.2
  114.1 1.6 copy-start
  118.3 4.8 copy-start.1
  123.1 1.4 copy-start.4
  124.5 1.0 copy-start.6
  125.4 0.8 copy-start.5
  125.4 1.5 copy-start.3
  126.9 1.2 copy-start.2
  133.6 1.6 copy-start
  137.9 4.8 copy-start.1
  142.7 1.4 copy-start.4
  144.0 1.0 copy-start.6
  145.0 0.8 copy-start.5
  145.0 1.5 copy-start.3
  146.5 1.2 copy-start.2
  153.2 1.6 copy-start
  157.4 4.8 copy-start.1
  162.2 1.4 copy-start.4
  163.6 1.0 copy-start.6
  164.5 0.8 copy-start.5
  164.5 1.5 copy-start.3
  166.1 1.2 copy-start.2
  172.8 1.6 copy-start
  177.0 4.8 copy-start.1
  181.8 1.4 copy-start.4
  183.1 1.0 copy-start.6
  184.1 0.8 copy-start.5
  184.1 1.5 copy-start.3
  185.6 1.2 copy-start.2
  192.3 1.6 copy-start
  196.5 4.7 copy-start.1
  201.3 1.4 copy-start.4
  202.7 1.0 copy-start.6
  203.6 0.8 copy-start.5
  203.6 1.5 copy-start.3
  205.2 224.2 %reduce-scatter.5.cloned.1.call-start = ((), (), s32[]{:S(2)}) async-start(), calls=%async_computation.3 | async-start | bytes 1179648 | tf_op jit(solution)/shard_map/reduce_scatter | solution.py:58
  205.9 286.8 %reduce-scatter.7.cloned.1.call-start = ((), (), s32[]{:S(2)}) async-start(), calls=%async_computation.5 | async-start | bytes 2228224
Sparse Core Ops, SparseCore 0:
  9.7 36.3 all-gather.1
  205.3 150.9 all-reduce.1
  360.8 68.4 reduce-scatter.4
  432.2 60.4 reduce-scatter.6
where the time goes:
time: 507 us; the launch traced here: 501 us
  waiting for transfers between devices  213 us (42%)
  blocking collectives  104 us (21%)
  local copies, waits for them, and re-layouts  91.2 us (18%)
  matrix products  68 us (13%)
  between operations  13.8 us (3%)
  other arithmetic  9.67 us (2%)
    psum x1, waiting for transfers between devices, per_device(): grad_weight, grad_bias = lax.psum((grad_w, grad_b), ('row', 'col'))  75.1 us
    reduce_scatter x1, waiting for transfers between devices, per_device(): lax.psum_scatter(grads_l.reshape(rows_i, S * C), 'col', scatter_dimension...  73.1 us
    psum x1, blocking collectives, per_device(): grad_weight, grad_bias = lax.psum((grad_w, grad_b), ('row', 'col'))  70.3 us
    unnamed x5, waiting for transfers between devices  64.7 us
    all_gather x1, blocking collectives, per_device(): left = lax.all_gather(left_proj, 'col', axis=0, tiled=True)  33.5 us
    convert_element_type x8, local copies, waits for them, and re-layouts, block(): jnp.dot(cot_flat, w_t, preferred_element_type=jnp.float32)  22.8 us
    dot_general x8, matrix products, block(): jnp.einsum('ijab,isa->jsb', d_four, left_blk, preferred_element_type=jnp....  21.1 us
    dot_general x8, matrix products, block(): jnp.dot(cot_flat, w_t, preferred_element_type=jnp.float32)  16 us
  transfers between devices with their start and end apart: 4, of which 4 were waited for; matrix products, arithmetic and copies ran while one was open for 2% of the time, Pallas kernels for 0%

commit v1 on v0

v1 whole, which is shorter than its diff:
```python
import functools

import jax
import jax.numpy as jnp
from jax import lax
from jax.experimental import pallas as pl
from jax.experimental.pallas import tpu as pltpu
from jax.sharding import PartitionSpec as P

C = 32
CZ = 128
S = 128
ROWS = 16
COLS = 8
TI = 64
TJ = 128
OWN = 8
MESH = pl.DeviceIdType.MESH
NN = (((1,), (0,)), ((), ()))
NT = (((1,), (1,)), ((), ()))
F32 = jnp.float32
BF16 = jnp.bfloat16


def dot(a, b, dims=NN):
    return lax.dot_general(a, b, dims, preferred_element_type=F32)


def kernel(
    a_ref, b_ref, w_ref, bias_ref, cot_hbm,
    pair_hbm, gl_ref, gr_ref, gw_ref, gb_ref,
    cot, d, p, a_all, a_t, b_in, b_all, b_t, w_t, pair,
    l_out, l_in, r_out, r_in, w1_out, w1_in, w2_out, w2_in, w3_out, w3_in, w4_in,
    cot_sem, pair_sem, a_s, a_r, b_s, b_r, l_s, l_r, r_s, r_r,
    w1_s, w1_r, w2_s, w2_r, w3_s, w3_r, w4_s, w4_r,
):
    row = lax.axis_index("row")
    col = lax.axis_index("col")

    def to_col(k, src, dst, ss, rs):
        return pltpu.make_async_remote_copy(
            src_ref=src, dst_ref=dst, send_sem=ss.at[k], recv_sem=rs.at[k],
            device_id=(row, lax.rem(col + k + 1, COLS)), device_id_type=MESH,
        )

    def to_row(k, src, dst, ss, rs):
        return pltpu.make_async_remote_copy(
            src_ref=src, dst_ref=dst, send_sem=ss.at[k], recv_sem=rs.at[k],
            device_id=(lax.rem(row + k + 1, ROWS), col), device_id_type=MESH,
        )

    def each(n, f):
        def step(k, carry):
            f(k)
            return carry

        lax.fori_loop(0, n, step, 0)

    def cot_copy(q):
        part = pl.ds(q * 16, 16)
        return pltpu.make_async_copy(cot_hbm.at[part], cot.at[part], cot_sem.at[q])

    def pair_copy(q):
        part = pl.ds(q * 16, 16)
        return pltpu.make_async_copy(pair.at[part], pair_hbm.at[part], pair_sem.at[q])

    each(4, lambda q: cot_copy(q).start())

    barrier = pltpu.get_barrier_semaphore()

    def greet_col(k):
        pl.semaphore_signal(barrier, inc=1, device_id=(row, lax.rem(col + k + 1, COLS)), device_id_type=MESH)

    def greet_row(k):
        pl.semaphore_signal(barrier, inc=1, device_id=(lax.rem(row + k + 1, ROWS), col), device_id_type=MESH)

    each(COLS - 1, greet_col)
    each(ROWS - 1, greet_row)
    pl.semaphore_wait(barrier, COLS + ROWS - 2)

    def send_b(k):
        to_row(k, b_ref, b_in.at[row], b_s, b_r).start()

    def send_a(k):
        to_col(k, a_ref, a_all.at[col], a_s, a_r).start()

    each(ROWS - 1, send_b)
    each(COLS - 1, send_a)
    a_all[col] = a_ref[...]
    b_in[row] = b_ref[...]
    w_t[...] = w_ref[...].T

    gb_ref[...] = jnp.zeros_like(gb_ref)
    group = 4

    def d_step(g, carry):
        @pl.when(lax.rem(g, 4) == 0)
        def _():
            cot_copy(g // 4).wait()

        block = cot[pl.ds(g * group, group)].reshape(group * TJ, CZ)
        r = dot(w_ref[...], block, NT).astype(BF16)
        for q in range(group):
            d[:, pl.ds((g * group + q) * C, C), :] = r[:, q * TJ:(q + 1) * TJ].reshape(C, C, TJ)
        gb_ref[...] += jnp.sum(block.astype(F32).reshape(group * TJ // 8, 8, CZ), axis=0)
        return carry

    lax.fori_loop(0, TI // group, d_step, 0)

    def wait_b(k):
        to_row(k, b_ref, b_in.at[lax.rem(row + ROWS - 1 - k, ROWS)], b_s, b_r).wait()

    def wait_a(k):
        to_col(k, a_ref, a_all.at[lax.rem(col + COLS - 1 - k, COLS)], a_s, a_r).wait()

    each(ROWS - 1, wait_b)
    each(COLS - 1, wait_a)

    def lay_b(q, carry):
        part = b_in[:, pl.ds(q * 16, 16), :].astype(F32)
        for h in range(2):
            b_all[pl.ds((q * 2 + h) * TJ, TJ), :] = part[:, h * 8:(h + 1) * 8, :].reshape(TJ, S).astype(BF16)
        return carry

    lax.fori_loop(0, C // 2, lay_b, 0)
    for q in range(COLS):
        a_t[:, q * 256:(q + 1) * 256] = a_all[q].T

    def p_step(n, carry):
        rhs = b_all[pl.ds(n * 512, 512), :]
        for m in range(4):
            r = dot(a_all[m * 2:m * 2 + 2].reshape(512, S), rhs, NT).astype(BF16)
            for q in range(4):
                p[n * 4 + q, m * 512:(m + 1) * 512, :] = r[:, q * TJ:(q + 1) * TJ]
        return carry

    lax.fori_loop(0, C * TJ // 512, p_step, 0)

    gw_ref[...] = jnp.zeros_like(gw_ref)

    def gw_step(g, carry):
        x = jnp.concatenate(
            [p[:, pl.ds((g * 8 + q) * C, C), :].reshape(C * C, TJ) for q in range(8)], axis=1
        )
        gw_ref[...] += dot(x, cot[pl.ds(g * 8, 8)].reshape(8 * TJ, CZ))
        return carry

    lax.fori_loop(0, TI // 8, gw_step, 0)
    for q in range(COLS):
        w1_out[q, :128, :] = gw_ref[q * 128:(q + 1) * 128, :]
        w1_out[q, 128:, :] = gb_ref[...]

    def send_w1(k):
        to_col(k, w1_out.at[lax.rem(col + k + 1, COLS)], w1_in.at[col], w1_s, w1_r).start()

    each(COLS - 1, send_w1)
    w1_in[col] = w1_out[col]

    def gr_step(n, carry):
        x = jnp.concatenate([d[n * 4 + q] for q in range(4)], axis=1)
        r = dot(a_t[...], x)
        t = [r[:, q * TJ:(q + 1) * TJ].T.reshape(ROWS, 8, S) for q in range(4)]
        for h in range(2):
            both = jnp.concatenate([t[2 * h], t[2 * h + 1]], axis=1)
            r_out[:, pl.ds(n * 32 + h * 16, 16), :] = both.astype(BF16)
        return carry

    lax.fori_loop(0, C // 4, gr_step, 0)

    def send_r(k):
        to_row(k, r_out.at[lax.rem(row + k + 1, ROWS)], r_in.at[row], r_s, r_r).start()

    each(ROWS - 1, send_r)
    r_in[row] = r_out[row]

    def wait_w1(k):
        to_col(k, w1_out.at[lax.rem(col + k + 1, COLS)], w1_in.at[lax.rem(col + COLS - 1 - k, COLS)], w1_s, w1_r).wait()

    each(COLS - 1, wait_w1)
    s1 = w1_in[0]
    for q in range(1, COLS):
        s1 += w1_in[q]
    for q in range(ROWS):
        w2_out[q, :8, :] = s1[q * 8:(q + 1) * 8, :]
        w2_out[q, 8:, :] = s1[128:, :]

    def send_w2(k):
        to_row(k, w2_out.at[lax.rem(row + k + 1, ROWS)], w2_in.at[row], w2_s, w2_r).start()

    each(ROWS - 1, send_w2)
    w2_in[row] = w2_out[row]

    def gl_step(m, carry):
        x = jnp.concatenate([d[q, pl.ds(m * 512, 512), :] for q in range(C)], axis=1)
        r = (dot(x, b_all[...]) * (1.0 / S)).astype(BF16)
        for h in range(2):
            l_out[m * 2 + h] = r[h * 256:(h + 1) * 256, :]
        return carry

    lax.fori_loop(0, TI * C // 512, gl_step, 0)

    def send_l(k):
        to_col(k, l_out.at[lax.rem(col + k + 1, COLS)], l_in.at[col], l_s, l_r).start()

    each(COLS - 1, send_l)
    l_in[col] = l_out[col]

    def wait_w2(k):
        to_row(k, w2_out.at[lax.rem(row + k + 1, ROWS)], w2_in.at[lax.rem(row + ROWS - 1 - k, ROWS)], w2_s, w2_r).wait()

    each(ROWS - 1, wait_w2)
    s2 = w2_in[0]
    for q in range(1, ROWS):
        s2 += w2_in[q]
    w3_out[...] = s2[:8, :]
    gb_ref[...] = s2[8:, :]

    def send_w3(k):
        to_row(k, w3_out, w3_in.at[row], w3_s, w3_r).start()

    each(ROWS - 1, send_w3)
    w3_in[row] = w3_out[...]

    def pair_step(g, carry):
        x = jnp.concatenate(
            [p[:, pl.ds((g * 4 + q) * C, C), :].reshape(C * C, TJ) for q in range(4)], axis=1
        )
        r = dot(w_t[...], x)
        for q in range(4):
            pair[g * 4 + q] = (r[:, q * TJ:(q + 1) * TJ].T + bias_ref[...]).astype(BF16)
        return carry

    for q in range(2):
        lax.fori_loop(q * 4, q * 4 + 4, pair_step, 0)
        pair_copy(q).start()

    def wait_r(k):
        to_row(k, r_out.at[lax.rem(row + k + 1, ROWS)], r_in.at[lax.rem(row + ROWS - 1 - k, ROWS)], r_s, r_r).wait()

    each(ROWS - 1, wait_r)
    total = r_in[0].astype(F32)
    for q in range(1, ROWS):
        total += r_in[q].astype(F32)
    gr_ref[...] = total

    def wait_w3(k):
        to_row(k, w3_out, w3_in.at[lax.rem(row + ROWS - 1 - k, ROWS)], w3_s, w3_r).wait()

    each(ROWS - 1, wait_w3)

    def send_w4(k):
        to_col(k, w3_in, w4_in.at[col], w4_s, w4_r).start()

    each(COLS - 1, send_w4)
    w4_in[col] = w3_in[...]

    for q in range(2, 4):
        lax.fori_loop(q * 4, q * 4 + 4, pair_step, 0)
        pair_copy(q).start()

    def wait_l(k):
        to_col(k, l_out.at[lax.rem(col + k + 1, COLS)], l_in.at[lax.rem(col + COLS - 1 - k, COLS)], l_s, l_r).wait()

    each(COLS - 1, wait_l)
    total = l_in[0].astype(F32)
    for q in range(1, COLS):
        total += l_in[q].astype(F32)
    gl_ref[...] = total

    def wait_w4(k):
        to_col(k, w3_in, w4_in.at[lax.rem(col + COLS - 1 - k, COLS)], w4_s, w4_r).wait()

    each(COLS - 1, wait_w4)
    gw_ref[...] = w4_in[...].reshape(C * C, CZ)
    each(4, lambda q: pair_copy(q).wait())


def per_device(left_proj, right_proj, out_weight, out_bias, pair_cotangent):
    a = (left_proj * BF16(1.0 / S)).reshape(OWN, S, C).transpose(0, 2, 1).reshape(OWN * C, S)
    b = right_proj.reshape(OWN, S, C).transpose(2, 0, 1).reshape(C * OWN, S)
    w = out_weight.reshape(C, C, CZ).transpose(1, 0, 2).reshape(C * C, CZ)
    vmem = pl.BlockSpec(memory_space=pltpu.VMEM)
    hbm = pl.BlockSpec(memory_space=pl.ANY)
    dma = pltpu.SemaphoreType.DMA
    own = OWN * C
    pair, gl, gr, gw, gb = pl.pallas_call(
        kernel,
        out_shape=(
            jax.ShapeDtypeStruct((TI, TJ, CZ), BF16),
            jax.ShapeDtypeStruct((own, S), F32),
            jax.ShapeDtypeStruct((own, S), F32),
            jax.ShapeDtypeStruct((C * C, CZ), F32),
            jax.ShapeDtypeStruct((8, CZ), F32),
        ),
        in_specs=[vmem, vmem, vmem, vmem, hbm],
        out_specs=(hbm, vmem, vmem, vmem, vmem),
        scratch_shapes=[
            pltpu.VMEM((TI, TJ, CZ), BF16),
            pltpu.VMEM((C, TI * C, TJ), BF16),
            pltpu.VMEM((C, TI * C, TJ), BF16),
            pltpu.VMEM((COLS, own, S), BF16),
            pltpu.VMEM((S, TI * C), BF16),
            pltpu.VMEM((ROWS, own, S), BF16),
            pltpu.VMEM((C * TJ, S), BF16),
            pltpu.VMEM((S, C * TJ), BF16),
            pltpu.VMEM((CZ, C * C), BF16),
            pltpu.VMEM((TI, TJ, CZ), BF16),
            pltpu.VMEM((COLS, own, S), BF16),
            pltpu.VMEM((COLS, own, S), BF16),
            pltpu.VMEM((ROWS, own, S), BF16),
            pltpu.VMEM((ROWS, own, S), BF16),
            pltpu.VMEM((COLS, 136, CZ), F32),
            pltpu.VMEM((COLS, 136, CZ), F32),
            pltpu.VMEM((ROWS, 16, CZ), F32),
            pltpu.VMEM((ROWS, 16, CZ), F32),
            pltpu.VMEM((8, CZ), F32),
            pltpu.VMEM((ROWS, 8, CZ), F32),
            pltpu.VMEM((COLS, ROWS, 8, CZ), F32),
            dma((4,)), dma((4,)),
            dma((COLS - 1,)), dma((COLS - 1,)), dma((ROWS - 1,)), dma((ROWS - 1,)),
            dma((COLS - 1,)), dma((COLS - 1,)), dma((ROWS - 1,)), dma((ROWS - 1,)),
            dma((COLS - 1,)), dma((COLS - 1,)), dma((ROWS - 1,)), dma((ROWS - 1,)),
            dma((ROWS - 1,)), dma((ROWS - 1,)), dma((COLS - 1,)), dma((COLS - 1,)),
        ],
        compiler_params=pltpu.CompilerParams(
            collective_id=0, has_side_effects=True, vmem_limit_bytes=60 << 20
        ),
        name="outer_product_mean",
    )(a, b, w, out_bias.reshape(1, CZ), pair_cotangent)
    grad_left = gl.reshape(OWN, C, S).transpose(0, 2, 1).reshape(OWN, S * C)
    grad_right = gr.reshape(C, OWN, S).transpose(1, 2, 0).reshape(OWN, S * C)
    grad_weight = gw.reshape(C, C, CZ).transpose(1, 0, 2).reshape(C * C, CZ)
    return pair, grad_left, grad_right, grad_weight, jnp.sum(gb, axis=0)


def solution(mesh):
    return jax.shard_map(
        per_device,
        mesh=mesh,
        in_specs=(
            P(("row", "col"), None),
            P(("col", "row"), None),
            P(),
            P(),
            P("row", "col", None),
        ),
        out_specs=(
            P("row", "col", None),
            P(("row", "col"), None),
            P(("col", "row"), None),
            P(),
            P(),
        ),
        check_vma=False,
    )
```

time: 507 us -> 94.4 us (0.19); the launches traced: 501 us -> 93.8 us
  waiting for transfers between devices: 213 us -> 0 us
  blocking collectives: 104 us -> 0 us
  local copies, waits for them, and re-layouts: 91.2 us -> 10.9 us
  Pallas kernels: 0 us -> 80 us
  matrix products: 68 us -> 0 us
  between operations: 13.8 us -> 0.69 us
  other arithmetic: 9.67 us -> 2.2 us
    pallas_call x0 -> x1, Pallas kernels: none -> 80 us  [per_device(): pl.pallas_call(kernel, out_shape=(jax.ShapeDtypeStruct((TI, TJ, CZ), BF16...]
    psum x1 -> x0, waiting for transfers between devices: 75.1 us -> none  [per_device(): grad_weight, grad_bias = lax.psum((grad_w, grad_b), ('row', 'col'))]
    reduce_scatter x1 -> x0, waiting for transfers between devices: 73.1 us -> none  [per_device(): lax.psum_scatter(grads_l.reshape(rows_i, S * C), 'col', scatter_dimension...]
    psum x1 -> x0, blocking collectives: 70.3 us -> none  [per_device(): grad_weight, grad_bias = lax.psum((grad_w, grad_b), ('row', 'col'))]
    dot_general x48 -> x0, matrix products: 68 us -> none  [the longest x8 21.1 us: block(): jnp.einsum('ijab,isa->jsb', d_four, left_blk, preferred_element_type=jnp....]
    unnamed x5 -> x0, waiting for transfers between devices: 64.7 us -> none
    convert_element_type x16 -> x0, local copies, waits for them, and re-layouts: 33.7 us -> none  [the longest x8 22.8 us: block(): jnp.dot(cot_flat, w_t, preferred_element_type=jnp.float32)]
    all_gather x1 -> x0, blocking collectives: 33.5 us -> none  [per_device(): left = lax.all_gather(left_proj, 'col', axis=0, tiled=True)]
  transfers between devices with their start and end apart: 4 -> 0, of which waited for: 4 -> 0; matrix products, arithmetic and copies ran while one was open for 2% -> 0% of each run, Pallas kernels for 0% -> 0%
where the time goes in v1:
time: 94.4 us; the launch traced here: 93.8 us
  Pallas kernels  80 us (85%)
  local copies, waits for them, and re-layouts  10.9 us (12%)
  other arithmetic  2.2 us (2%)
    pallas_call x1, Pallas kernels, per_device(): pl.pallas_call(kernel, out_shape=(jax.ShapeDtypeStruct((TI, TJ, CZ), BF16...  80 us
    reshape x2, local copies, waits for them, and re-layouts, per_device(): grad_right = gr.reshape(C, OWN, S).transpose(1, 2, 0).reshape(OWN, S * C)  1.99 us
    reshape x2, local copies, waits for them, and re-layouts, per_device(): grad_left = gl.reshape(OWN, C, S).transpose(0, 2, 1).reshape(OWN, S * C)  1.99 us

profile of v1, /device:TPU:1, one launch (start us, length us, event | category | flops | bytes accessed | tf_op | source)
XLA Modules:
  0.0 93.8 jit_solution(3260764367440655703)
XLA Ops:
  0.6 0.8 broadcast_multiply_fusion
  1.5 0.2 reshape.49
  1.7 0.8 copy.16
  2.4 1.1 %reshape.51 = bf16[8,128,32]{2,1,0:T(8,128)(2,1)S(1)} reshape(bf16[8,4096]{1,0:T(8,128)(2,1)} %param.6) | data formatting | bytes 131072 | tf_op jit(solution)/shard_map/reshape | solution.py:280
  3.5 0.8 copy.17
  4.3 1.8 %copy.18 = bf16[32,32,128]{2,0,1:T(8,128)(2,1)} copy(bf16[32,32,128]{2,1,0:T(8,128)(2,1)} %bitcast.26) | data formatting | bytes 524288 | tf_op jit(solution)/shard_map/reshape | solution.py:281
  6.0 80.0 %outer_product_mean.1 = (bf16[64,128,128]{2,1,0:T(8,128)(2,1)}, f32[256,128]{1,0:T(8,128)}, f32[256,128]{1,0:T(8,128)}, f32[1024,128]{1,0:T(8,128)}, f32[8,128]{1,0:T(8,128)}) custom-call(bf16[256,128]{1,0:T(8,128)(2,1)} %bitcast.24, bf16[256,128]{1,0:T(8,128)(2,1)} %bitcast.25, bf16[1024,128]{1,0:T(8,128)(2,1)} %bitcast.21, f32[1,128]{1,0:T(1,128)} %bitcast.29, ...), custom_call_target="tpu_custom_call" | custom-call | tf_op jit(solution)/shard_map/outer_product_mean/pallas_call | solution.py:286
  86.0 0.0 copy-start.1
  86.1 0.0 copy-start
  86.1 1.4 %reduce_sum.9 = f32[128]{0:T(128)} reduce(f32[8,128]{1,0:T(8,128)} %get-tuple-element.14, f32[]{:T(128)} %constant.1.clone.1), dimensions={0}, to_apply=%region_0.0 | reduce | flops 896 | bytes 4612 | tf_op jit(solution)/shard_map/reduce_sum | solution.py:333
  87.4 1.1 %copy.19 = f32[8,32,128]{1,2,0:T(8,128)S(1)} copy(f32[8,32,128]{2,1,0:T(8,128)} %bitcast.28) | data formatting | bytes 262144 | tf_op jit(solution)/shard_map/reshape | solution.py:330
  88.5 0.9 reshape.57
  89.4 1.1 %copy.20 = f32[32,8,128]{0,2,1:T(8,128)S(1)} copy(f32[32,8,128]{2,1,0:T(8,128)} %bitcast.27) | data formatting | bytes 262144 | tf_op jit(solution)/shard_map/reshape | solution.py:331
  90.5 0.9 reshape.59
  91.4 0.0 copy-done.1
  91.4 1.1 %copy.21 = f32[32,32,128]{2,1,0:T(8,128)} copy(f32[32,32,128]{2,0,1:T(8,128)S(1)} %bitcast.22) | data formatting | bytes 1048576 | tf_op jit(solution)/shard_map/transpose | solution.py:332
  92.5 0.0 copy-done
  92.5 1.3 %copy.23 = bf16[64,128,128]{2,1,0:T(8,128)(2,1)} copy(bf16[64,128,128]{2,1,0:T(8,128)(2,1)S(1)} %copy-done) | data formatting | bytes 4194304
Async XLA Ops:
  86.0 5.4 %copy-start.1 = (f32[1024,128]{1,0:T(8,128)S(1)}, f32[1024,128]{1,0:T(8,128)}, u32[]{:S(2)}) copy-start(f32[1024,128]{1,0:T(8,128)} %get-tuple-element.13) | copy-start | bytes 1572868
  86.1 6.5 %copy-start = (bf16[64,128,128]{2,1,0:T(8,128)(2,1)S(1)}, bf16[64,128,128]{2,1,0:T(8,128)(2,1)}, u32[]{:S(2)}) copy-start(bf16[64,128,128]{2,1,0:T(8,128)(2,1)} %get-tuple-element.20) | copy-start | bytes 6291460

commit v2 on v1

v2 whole, which is shorter than its diff:
```python
import functools

import jax
import jax.numpy as jnp
from jax import lax
from jax.experimental import pallas as pl
from jax.experimental.pallas import tpu as pltpu
from jax.sharding import PartitionSpec as P

C = 32
CZ = 128
S = 128
ROWS = 16
COLS = 8
TI = 64
TJ = 128
OWN = 8
MESH = pl.DeviceIdType.MESH
NN = (((1,), (0,)), ((), ()))
NT = (((1,), (1,)), ((), ()))
F32 = jnp.float32
BF16 = jnp.bfloat16


def dot(a, b, dims=NN):
    return lax.dot_general(a, b, dims, preferred_element_type=F32)


def kernel(
    a_ref, b_ref, w_ref, bias_ref, cot_hbm,
    pair_hbm, gl_ref, gr_ref, gw_ref, gb_ref,
    cot, d, p, a_all, a_t, b_in, b_all, w_t, pair,
    l_out, l_in, l_x, l_xin, r_keep, r_x, r_xin, r_out, r_in,
    w0, w0_in, w1_out, w1_in, w2_out, w2_in, w3_out, w3_in, w5,
    cot_sem, pair_sem, ax_s, ax_r, az_s, az_r, bc_s, bc_r, bx_s, bx_r, by_s, by_r,
    l_s, l_r, lx_s, lx_r, rx_s, rx_r, r_s, r_r,
    w0_s, w0_r, w1_s, w1_r, w2_s, w2_r, w3_s, w3_r, w4_s, w4_r, w5_s, w5_r,
):
    row = lax.axis_index("row")
    col = lax.axis_index("col")
    half = lax.div(row, 8)
    y = lax.rem(lax.div(row, 2), 4)
    core = lax.rem(row, 2)
    z = lax.div(col, 2)
    far = lax.rem(col, 2)
    mate = half * 8 + y * 2 + (1 - core)
    near = (1 - half) * 8 + y * 2 + core
    other = z * 2 + (1 - far)
    spot = half * 4 + y

    def row_y(n, h=None):
        return (half if h is None else h) * 8 + lax.rem(y + n + 4, 4) * 2 + core

    def col_z(n, f=None):
        return lax.rem(z + n + 4, 4) * 2 + (far if f is None else f)

    def row_spot(n):
        q = lax.rem(spot + n + 8, 8)
        return q, q * 2 + core

    def send(src, dst, ss, rs, k, r=None, c=None):
        return pltpu.make_async_remote_copy(
            src_ref=src, dst_ref=dst, send_sem=ss.at[k], recv_sem=rs.at[k],
            device_id=(row if r is None else r, col if c is None else c), device_id_type=MESH,
        )

    def each(n, f):
        def step(k, carry):
            f(k)
            return carry

        lax.fori_loop(0, n, step, 0)

    def cot_copy(q):
        part = pl.ds(q * 16, 16)
        return pltpu.make_async_copy(cot_hbm.at[part], cot.at[part], cot_sem.at[q])

    def pair_copy(q):
        part = pl.ds(q * 16, 16)
        return pltpu.make_async_copy(pair.at[part], pair_hbm.at[part], pair_sem.at[q])

    each(4, lambda q: cot_copy(q).start())

    barrier = pltpu.get_barrier_semaphore()

    def greet(r, c):
        pl.semaphore_signal(barrier, inc=1, device_id=(r, c), device_id_type=MESH)

    each(COLS - 1, lambda k: greet(row, lax.rem(col + k + 1, COLS)))
    each(7, lambda k: greet(row_spot(k + 1)[1], col))
    greet(mate, col)
    pl.semaphore_wait(barrier, 15)

    bx = send(b_ref, b_in.at[row], bx_s, bx_r, 0, r=near)
    bx.start()
    ax = send(a_ref, a_all.at[col], ax_s, ax_r, 0, c=other)
    ax.start()

    def by_own(k):
        return send(b_ref, b_in.at[row], by_s, by_r, k, r=row_y(k + 1))

    def az_own(k):
        return send(a_ref, a_all.at[col], az_s, az_r, k, c=col_z(k + 1))

    def by_near(k):
        return send(b_in.at[near], b_in.at[near], by_s, by_r, k + 3, r=row_y(k + 1))

    def az_other(k):
        return send(a_all.at[other], a_all.at[other], az_s, az_r, k + 3, c=col_z(k + 1))

    def bc_near():
        return send(b_in.at[near], b_in.at[near], bc_s, bc_r, 1, r=mate)

    def bc_y(k, h, first):
        slot = b_in.at[row_y(-1 - k, h)]
        return send(slot, slot, bc_s, bc_r, first + k, r=mate)

    bc_own = send(b_ref, b_in.at[row], bc_s, bc_r, 0, r=mate)
    each(3, lambda k: by_own(k).start())
    each(3, lambda k: az_own(k).start())
    bc_own.start()
    a_all[col] = a_ref[...]
    b_in[row] = b_ref[...]
    w_t[...] = w_ref[...].T

    def relay_x():
        send(b_ref, b_in.at[near], bx_s, bx_r, 0, r=near).wait_recv()
        each(3, lambda k: by_near(k).start())
        bc_near().start()
        send(a_ref, a_all.at[other], ax_s, ax_r, 0, c=other).wait_recv()
        each(3, lambda k: az_other(k).start())

    def relay_y(h, first, base):
        def step(k):
            slot = b_in.at[row_y(-1 - k, h)]
            send(b_ref, slot, by_s, by_r, base + k, r=row_y(k + 1)).wait_recv()
            bc_y(k, h, first).start()

        each(3, step)

    def end_a():
        def step(k):
            send(a_ref, a_all.at[col_z(-1 - k)], az_s, az_r, k, c=col_z(k + 1)).wait()
            send(a_ref, a_all.at[col_z(-1 - k, 1 - far)], az_s, az_r, k + 3, c=col_z(k + 1)).wait()

        each(3, step)
        ax.wait_send()

    def end_b():
        def from_mate(k, r):
            slot = r - core + (1 - core)
            send(b_ref, b_in.at[slot], bc_s, bc_r, k, r=mate).wait()

        from_mate(0, row)
        from_mate(1, near)
        each(3, lambda k: from_mate(k + 2, row_y(-1 - k)))
        each(3, lambda k: from_mate(k + 5, row_y(-1 - k, 1 - half)))
        bx.wait_send()
        each(6, lambda k: send(b_ref, b_in.at[row], by_s, by_r, k, r=near).wait_send())

    gb_ref[...] = jnp.zeros_like(gb_ref)
    group = 8

    def d_step(g, carry):
        @pl.when(lax.rem(g, 2) == 0)
        def _():
            cot_copy(lax.div(g, 2)).wait()

        block = cot[pl.ds(g * group, group)].reshape(group * TJ, CZ)
        r = dot(w_ref[...], block, NT).astype(BF16)
        for q in range(group):
            d[:, pl.ds((g * group + q) * C, C), :] = r[:, q * TJ:(q + 1) * TJ].reshape(C, C, TJ)
        gb_ref[...] += jnp.sum(block.astype(F32).reshape(group * TJ // 8, 8, CZ), axis=0)
        return carry

    lax.fori_loop(0, 3, d_step, 0)
    relay_x()
    lax.fori_loop(3, 6, d_step, 0)
    relay_y(half, 2, 0)
    lax.fori_loop(6, 8, d_step, 0)
    end_a()
    for q in range(COLS):
        a_t[:, q * 256:(q + 1) * 256] = a_all[q].T
    relay_y(1 - half, 5, 3)

    def rx(g):
        part = pl.ds(g * 64, 64)
        return send(r_x.at[:, part], r_xin.at[:, part], rx_s, rx_r, g, r=mate)

    def gr_step(g, carry):
        x = jnp.concatenate([d[g * 8 + q] for q in range(8)], axis=1)
        r = dot(a_t[...], x)
        t = [r[:, q * TJ:(q + 1) * TJ].T.reshape(8, 16, S) for q in range(8)]
        even = [jnp.where(core == 0, v[:, :8], v[:, 8:]) for v in t]
        odd = [jnp.where(core == 0, v[:, 8:], v[:, :8]) for v in t]
        r_keep[:, pl.ds(g * 64, 64), :] = jnp.concatenate(even, axis=1)
        for h in range(4):
            both = jnp.concatenate(odd[2 * h:2 * h + 2], axis=1)
            r_x[:, pl.ds(g * 64 + h * 16, 16), :] = both.astype(BF16)
        rx(g).start()
        return carry

    lax.fori_loop(0, C // 8, gr_step, 0)

    end_b()

    def lay_b(q, carry):
        part = b_in[:, pl.ds(q * 16, 16), :].astype(F32)
        for h in range(2):
            b_all[pl.ds((q * 2 + h) * TJ, TJ), :] = part[:, h * 8:(h + 1) * 8, :].reshape(TJ, S).astype(BF16)
        return carry

    lax.fori_loop(0, C // 2, lay_b, 0, unroll=4)

    def p_step(n, carry):
        rhs = b_all[pl.ds(n * 2048, 2048), :]
        for m in range(8):
            r = dot(a_all[m], rhs, NT).astype(BF16)
            for q in range(16):
                p[n * 16 + q, m * 256:(m + 1) * 256, :] = r[:, q * TJ:(q + 1) * TJ]
        return carry

    lax.fori_loop(0, 1, p_step, 0)

    def send_r(k):
        q, r = row_spot(k + 1)
        return send(r_out.at[q], r_in.at[spot], r_s, r_r, k, r=r)

    each(4, lambda g: rx(g).wait())

    def sum_x(q):
        r_out[q] = (r_keep[q] + r_xin[q].astype(F32)).astype(BF16)

    each(8, sum_x)
    each(7, lambda k: send_r(k).start())
    r_in[spot] = r_out[spot]

    lax.fori_loop(1, 2, p_step, 0)

    def gw_step(g, carry):
        x = jnp.concatenate(
            [p[pl.ds(g * 16, 16), q * C:(q + 1) * C, :].reshape(16 * C, TJ) for q in range(TI)], axis=1
        )
        w0[g, :512, :] = dot(x, cot[...].reshape(TI * TJ, CZ))
        return carry

    lax.fori_loop(0, 2, gw_step, 0)
    w0[0, 512:, :] = gb_ref[...]
    w0[1, 512:, :] = gb_ref[...]
    w0_copy = send(w0.at[1 - core], w0_in, w0_s, w0_r, 0, r=mate)
    w0_copy.start()

    def gl_step(m, carry):
        x = jnp.concatenate([d[q, pl.ds(m * 1024, 1024), :] for q in range(C)], axis=1)
        r = (dot(x, b_all[...]) * (1.0 / S)).astype(BF16)
        for h in range(4):
            l_out[m * 4 + h] = r[h * 256:(h + 1) * 256, :]
        return carry

    lax.fori_loop(0, 1, gl_step, 0)

    w0_copy.wait()
    for q in range(COLS):
        part = slice(q * 64, q * 64 + 64)
        w1_out[q, :64, :] = w0[core, part, :] + w0_in[part, :]
        w1_out[q, 64:, :] = w0[core, 512:, :] + w0_in[512:, :]

    def send_w1(k, slot):
        to = lax.rem(col + k + 1, COLS)
        return send(w1_out.at[to], w1_in.at[slot], w1_s, w1_r, k, c=to)

    each(COLS - 1, lambda k: send_w1(k, col).start())
    w1_in[col] = w1_out[col]

    lax.fori_loop(1, 2, gl_step, 0)

    def send_l(k):
        to = lax.rem(z + k + 1, 4)
        return send(l_out.at[pl.ds(to * 2, 2)], l_in.at[k], l_s, l_r, k, c=to * 2 + far)

    each(3, lambda k: send_l(k).start())

    each(COLS - 1, lambda k: send_w1(k, lax.rem(col + COLS - 1 - k, COLS)).wait())
    s1 = w1_in[0]
    for q in range(1, COLS):
        s1 += w1_in[q]
    for q in range(8):
        w2_out[q, :8, :] = s1[q * 8:(q + 1) * 8, :]
        w2_out[q, 8:, :] = s1[64:, :]

    def send_w2(k, slot):
        q, r = row_spot(k + 1)
        return send(w2_out.at[q], w2_in.at[slot], w2_s, w2_r, k, r=r)

    each(7, lambda k: send_w2(k, spot).start())
    w2_in[spot] = w2_out[spot]

    def pair_step(g, carry):
        x = jnp.concatenate(
            [p[:, pl.ds((g * 16 + q) * C, C), :].reshape(C * C, TJ) for q in range(16)], axis=1
        )
        r = dot(w_t[...], x)
        for q in range(16):
            pair[g * 16 + q] = (r[:, q * TJ:(q + 1) * TJ].T + bias_ref[...]).astype(BF16)
        pair_copy(g).start()
        return carry

    lax.fori_loop(0, 1, pair_step, 0)

    each(7, lambda k: send_w2(k, row_spot(-1 - k)[0]).wait())
    s2 = w2_in[0]
    for q in range(1, 8):
        s2 += w2_in[q]
    w3_out[...] = s2[:8, :]
    gb_ref[...] = s2[8:, :]

    def send_w3(k, slot):
        return send(w3_out, w3_in.at[slot], w3_s, w3_r, k, r=row_spot(k + 1)[1])

    each(7, lambda k: send_w3(k, spot).start())
    w3_in[spot] = w3_out[...]

    lax.fori_loop(1, 2, pair_step, 0)

    each(3, lambda k: send_l(k).wait())
    mine = l_out[pl.ds(z * 2 + far, 1)][0].astype(F32)
    theirs = l_out[pl.ds(z * 2 + 1 - far, 1)][0].astype(F32)
    for k in range(3):
        mine += l_in[k, far].astype(F32)
        theirs += l_in[k, 1 - far].astype(F32)
    l_x[...] = theirs.astype(BF16)
    lx = send(l_x, l_xin, lx_s, lx_r, 0, c=other)
    lx.start()
    gl_ref[...] = mine

    each(7, lambda k: send_w3(k, row_spot(-1 - k)[0]).wait())

    def send_w4(k, slot):
        return send(w3_in, w5.at[core, slot], w4_s, w4_r, k, c=lax.rem(col + k + 1, COLS))

    each(COLS - 1, lambda k: send_w4(k, col).start())
    w5[core, col] = w3_in[...]

    lax.fori_loop(2, 4, pair_step, 0)

    each(7, lambda k: send(r_out.at[0], r_in.at[row_spot(-1 - k)[0]], r_s, r_r, k, r=near).wait())
    total = r_in[0].astype(F32)
    for q in range(1, 8):
        total += r_in[q].astype(F32)
    gr_ref[...] = total

    each(COLS - 1, lambda k: send_w4(k, lax.rem(col + COLS - 1 - k, COLS)).wait())
    send(w5.at[core], w5.at[core], w5_s, w5_r, 0, r=mate).start()
    lx.wait()
    gl_ref[...] += l_xin[...].astype(F32)
    send(w5.at[core], w5.at[1 - core], w5_s, w5_r, 0, r=mate).wait()
    gw_ref[...] = w5[...].reshape(C * C, CZ)
    each(4, lambda q: pair_copy(q).wait())


def per_device(left_proj, right_proj, out_weight, out_bias, pair_cotangent):
    a = (left_proj * BF16(1.0 / S)).reshape(OWN, S, C).transpose(0, 2, 1).reshape(OWN * C, S)
    b = right_proj.reshape(OWN, S, C).transpose(2, 0, 1).reshape(C * OWN, S)
    w = out_weight.reshape(C, C, CZ).transpose(1, 0, 2).reshape(C * C, CZ)
    vmem = pl.BlockSpec(memory_space=pltpu.VMEM)
    hbm = pl.BlockSpec(memory_space=pl.ANY)
    dma = pltpu.SemaphoreType.DMA
    own = OWN * C
    pair, gl, gr, gw, gb = pl.pallas_call(
        kernel,
        out_shape=(
            jax.ShapeDtypeStruct((TI, TJ, CZ), BF16),
            jax.ShapeDtypeStruct((own, S), F32),
            jax.ShapeDtypeStruct((own, S), F32),
            jax.ShapeDtypeStruct((C * C, CZ), F32),
            jax.ShapeDtypeStruct((8, CZ), F32),
        ),
        in_specs=[vmem, vmem, vmem, vmem, hbm],
        out_specs=(hbm, vmem, vmem, vmem, vmem),
        scratch_shapes=[
            pltpu.VMEM((TI, TJ, CZ), BF16),
            pltpu.VMEM((C, TI * C, TJ), BF16),
            pltpu.VMEM((C, TI * C, TJ), BF16),
            pltpu.VMEM((COLS, own, S), BF16),
            pltpu.VMEM((S, TI * C), BF16),
            pltpu.VMEM((ROWS, own, S), BF16),
            pltpu.VMEM((C * TJ, S), BF16),
            pltpu.VMEM((CZ, C * C), BF16),
            pltpu.VMEM((TI, TJ, CZ), BF16),
            pltpu.VMEM((COLS, own, S), BF16),
            pltpu.VMEM((3, 2, own, S), BF16),
            pltpu.VMEM((own, S), BF16),
            pltpu.VMEM((own, S), BF16),
            pltpu.VMEM((8, own, S), F32),
            pltpu.VMEM((8, own, S), BF16),
            pltpu.VMEM((8, own, S), BF16),
            pltpu.VMEM((8, own, S), BF16),
            pltpu.VMEM((8, own, S), BF16),
            pltpu.VMEM((2, 520, CZ), F32),
            pltpu.VMEM((520, CZ), F32),
            pltpu.VMEM((COLS, 72, CZ), F32),
            pltpu.VMEM((COLS, 72, CZ), F32),
            pltpu.VMEM((8, 16, CZ), F32),
            pltpu.VMEM((8, 16, CZ), F32),
            pltpu.VMEM((8, CZ), F32),
            pltpu.VMEM((8, 8, CZ), F32),
            pltpu.VMEM((2, COLS, 8, 8, CZ), F32),
            dma((4,)), dma((4,)),
            dma((1,)), dma((1,)), dma((6,)), dma((6,)),
            dma((8,)), dma((8,)), dma((1,)), dma((1,)), dma((6,)), dma((6,)),
            dma((3,)), dma((3,)), dma((1,)), dma((1,)),
            dma((4,)), dma((4,)), dma((7,)), dma((7,)),
            dma((1,)), dma((1,)), dma((7,)), dma((7,)), dma((7,)), dma((7,)),
            dma((7,)), dma((7,)), dma((7,)), dma((7,)), dma((1,)), dma((1,)),
        ],
        compiler_params=pltpu.CompilerParams(
            collective_id=0, has_side_effects=True, vmem_limit_bytes=60 << 20
        ),
        name="outer_product_mean",
    )(a, b, w, out_bias.reshape(1, CZ), pair_cotangent)
    grad_left = gl.reshape(OWN, C, S).transpose(0, 2, 1).reshape(OWN, S * C)
    grad_right = gr.reshape(C, OWN, S).transpose(1, 2, 0).reshape(OWN, S * C)
    grad_weight = gw.reshape(C, C, CZ).transpose(1, 0, 2).reshape(C * C, CZ)
    return pair, grad_left, grad_right, grad_weight, jnp.sum(gb, axis=0)


def solution(mesh):
    return jax.shard_map(
        per_device,
        mesh=mesh,
        in_specs=(
            P(("row", "col"), None),
            P(("col", "row"), None),
            P(),
            P(),
            P("row", "col", None),
        ),
        out_specs=(
            P("row", "col", None),
            P(("row", "col"), None),
            P(("col", "row"), None),
            P(),
            P(),
        ),
        check_vma=False,
    )
```

time: 94.4 us -> 74.3 us (0.79)
  Pallas kernels: 80 us -> 60.2 us
    pallas_call x1, Pallas kernels: 80 us -> 60.2 us  [per_device(): pl.pallas_call(kernel, out_shape=(jax.ShapeDtypeStruct((TI, TJ, CZ), BF16...]
where the time goes in v2:
time: 74.3 us; the launch traced here: 74 us
  Pallas kernels  60.2 us (81%)
  local copies, waits for them, and re-layouts  10.9 us (15%)
  other arithmetic  2.2 us (3%)
    pallas_call x1, Pallas kernels, per_device(): pl.pallas_call(kernel, out_shape=(jax.ShapeDtypeStruct((TI, TJ, CZ), BF16...  60.2 us
    reshape x2, local copies, waits for them, and re-layouts, per_device(): grad_right = gr.reshape(C, OWN, S).transpose(1, 2, 0).reshape(OWN, S * C)  1.99 us
    reshape x2, local copies, waits for them, and re-layouts, per_device(): grad_left = gl.reshape(OWN, C, S).transpose(0, 2, 1).reshape(OWN, S * C)  1.99 us
    reshape x1, local copies, waits for them, and re-layouts, per_device(): w = out_weight.reshape(C, C, CZ).transpose(1, 0, 2).reshape(C * C, CZ)  1.76 us

profile of v2, /device:TPU:1, one launch (start us, length us, event | category | flops | bytes accessed | tf_op | source)
XLA Modules:
  0.0 74.0 jit_solution(5738833486741359740)
XLA Ops:
  0.6 0.8 %broadcast_multiply_fusion = bf16[8,4096]{1,0:T(8,128)(2,1)S(1)} fusion(bf16[8,4096]{1,0:T(8,128)(2,1)} %param.5), kind=kLoop, calls=%fused_computation | loop fusion | flops 32768 | bytes 131072 | tf_op jit(solution)/shard_map/mul | solution.py:362
  1.5 0.2 reshape.49
  1.7 0.8 %copy.16 = bf16[8,32,128]{2,1,0:T(8,128)(2,1)} copy(bf16[8,32,128]{1,2,0:T(8,128)(2,1)S(1)} %bitcast.19) | data formatting | bytes 131072 | tf_op jit(solution)/shard_map/transpose | solution.py:362
  2.4 1.1 %reshape.51 = bf16[8,128,32]{2,1,0:T(8,128)(2,1)S(1)} reshape(bf16[8,4096]{1,0:T(8,128)(2,1)} %param.6) | data formatting | bytes 131072 | tf_op jit(solution)/shard_map/reshape | solution.py:363
  3.5 0.8 %copy.17 = bf16[32,8,128]{2,1,0:T(8,128)(2,1)} copy(bf16[32,8,128]{0,2,1:T(8,128)(2,1)S(1)} %bitcast.20) | data formatting | bytes 131072 | tf_op jit(solution)/shard_map/transpose | solution.py:363
  4.3 1.8 %copy.18 = bf16[32,32,128]{2,0,1:T(8,128)(2,1)} copy(bf16[32,32,128]{2,1,0:T(8,128)(2,1)} %bitcast.26) | data formatting | bytes 524288 | tf_op jit(solution)/shard_map/reshape | solution.py:364
  6.0 60.2 %outer_product_mean.1 = (bf16[64,128,128]{2,1,0:T(8,128)(2,1)}, f32[256,128]{1,0:T(8,128)}, f32[256,128]{1,0:T(8,128)}, f32[1024,128]{1,0:T(8,128)}, f32[8,128]{1,0:T(8,128)}) custom-call(bf16[256,128]{1,0:T(8,128)(2,1)} %bitcast.24, bf16[256,128]{1,0:T(8,128)(2,1)} %bitcast.25, bf16[1024,128]{1,0:T(8,128)(2,1)} %bitcast.21, f32[1,128]{1,0:T(1,128)} %bitcast.29, ...), custom_call_target="tpu_custom_call" | custom-call | tf_op jit(solution)/shard_map/outer_product_mean/pallas_call | solution.py:369
  66.2 0.0 copy-start.1
  66.2 0.0 copy-start
  66.3 1.4 %reduce_sum.9 = f32[128]{0:T(128)} reduce(f32[8,128]{1,0:T(8,128)} %get-tuple-element.14, f32[]{:T(128)} %constant.1.clone.1), dimensions={0}, to_apply=%region_0.0 | reduce | flops 896 | bytes 4612 | tf_op jit(solution)/shard_map/reduce_sum | solution.py:424
  67.6 1.1 %copy.19 = f32[8,32,128]{1,2,0:T(8,128)S(1)} copy(f32[8,32,128]{2,1,0:T(8,128)} %bitcast.28) | data formatting | bytes 262144 | tf_op jit(solution)/shard_map/reshape | solution.py:421
  68.7 0.9 %reshape.57 = f32[8,4096]{1,0:T(8,128)} reshape(f32[8,128,32]{2,1,0:T(8,128)S(1)} %bitcast.17) | data formatting | bytes 262144 | tf_op jit(solution)/shard_map/reshape | solution.py:421
  69.6 1.1 %copy.20 = f32[32,8,128]{0,2,1:T(8,128)S(1)} copy(f32[32,8,128]{2,1,0:T(8,128)} %bitcast.27) | data formatting | bytes 262144 | tf_op jit(solution)/shard_map/reshape | solution.py:422
  70.7 0.9 %reshape.59 = f32[8,4096]{1,0:T(8,128)} reshape(f32[8,128,32]{2,1,0:T(8,128)S(1)} %bitcast.18) | data formatting | bytes 262144 | tf_op jit(solution)/shard_map/reshape | solution.py:422
  71.6 0.0 copy-done.1
  71.6 1.1 %copy.21 = f32[32,32,128]{2,1,0:T(8,128)} copy(f32[32,32,128]{2,0,1:T(8,128)S(1)} %bitcast.22) | data formatting | bytes 1048576 | tf_op jit(solution)/shard_map/transpose | solution.py:423
  72.7 0.0 copy-done
  72.7 1.3 %copy.23 = bf16[64,128,128]{2,1,0:T(8,128)(2,1)} copy(bf16[64,128,128]{2,1,0:T(8,128)(2,1)S(1)} %copy-done) | data formatting | bytes 4194304
Async XLA Ops:
  66.2 5.4 %copy-start.1 = (f32[1024,128]{1,0:T(8,128)S(1)}, f32[1024,128]{1,0:T(8,128)}, u32[]{:S(2)}) copy-start(f32[1024,128]{1,0:T(8,128)} %get-tuple-element.13) | copy-start | bytes 1572868
  66.2 6.5 %copy-start = (bf16[64,128,128]{2,1,0:T(8,128)(2,1)S(1)}, bf16[64,128,128]{2,1,0:T(8,128)(2,1)}, u32[]{:S(2)}) copy-start(bf16[64,128,128]{2,1,0:T(8,128)(2,1)} %get-tuple-element.20) | copy-start | bytes 6291460

commit v3 on v2

--- a/solution.py
+++ b/solution.py
@@ -14,6 +14,7 @@
 COLS = 8
 TI = 64
 TJ = 128
+CHIPS = 64
 OWN = 8
 MESH = pl.DeviceIdType.MESH
 NN = (((1,), (0,)), ((), ()))
@@ -26,15 +27,78 @@
     return lax.dot_general(a, b, dims, preferred_element_type=F32)
 
 
+def swap(parts):
+    block = lax.broadcasted_iota(jnp.int32, (C, S), 1) // C
+    out = []
+    for n in range(4):
+        v = None
+        for m in range(4):
+            r = parts[m] if m == n else pltpu.roll(parts[m], (m - n) * C % S, 1)
+            v = r if v is None else jnp.where(block == m, r, v)
+        out.append(v)
+    return out
+
+
+def prepare(left_ref, right_ref, weight_ref, a_ref, b_ref, w_ref, stage, flat):
+    for n, ref in enumerate((left_ref, right_ref)):
+        for q in range(C):
+            stage[n, q * OWN:(q + 1) * OWN, :] = ref[:, q * S:(q + 1) * S].astype(F32)
+    for n in range(2):
+        for g in range(2):
+            x = jnp.concatenate([stage[n, pl.ds(g * 4 + i, C, stride=OWN), :] for i in range(4)], axis=0)
+            t = x.T
+            parts = swap([t[m * C:(m + 1) * C] for m in range(4)])
+            for i in range(4):
+                if n == 0:
+                    a_ref[(g * 4 + i) * C:(g * 4 + i + 1) * C, :] = (parts[i] * (1.0 / S)).astype(BF16)
+                else:
+                    flat[pl.ds(g * 4 + i, C, stride=OWN), :] = parts[i]
+    b_ref[...] = flat[:OWN * C, :].astype(BF16)
+    flat[...] = weight_ref[...].astype(F32)
+    for c in range(C):
+        w_ref[c * C:(c + 1) * C, :] = flat[pl.ds(c, C, stride=C), :].astype(BF16)
+
+
+def finish(
+    gl_ref, gr_ref, gw_ref, gb_ref, pair_in,
+    left_ref, right_ref, weight_ref, bias_ref, pair_out, hold, stage, in_sem, out_sem,
+):
+    def part(ref, q):
+        return ref.at[pl.ds(q * 16, 16)]
+
+    load = [pltpu.make_async_copy(part(pair_in, q), part(hold, q), in_sem.at[q]) for q in range(4)]
+    save = [pltpu.make_async_copy(part(hold, q), part(pair_out, q), out_sem.at[q]) for q in range(4)]
+    for c in load:
+        c.start()
+    for n, (ref, out) in enumerate(((gl_ref, left_ref), (gr_ref, right_ref))):
+        for g in range(2):
+            rows = [
+                ref[(g * 4 + i) * C:(g * 4 + i + 1) * C, :] if n == 0
+                else ref[pl.ds(g * 4 + i, C, stride=OWN), :]
+                for i in range(4)
+            ]
+            stage[n, g * S:(g + 1) * S, :] = jnp.concatenate(swap(rows), axis=0).T
+    for q in range(4):
+        load[q].wait()
+        save[q].start()
+    for n, out in enumerate((left_ref, right_ref)):
+        for q in range(C):
+            out[:, q * S:(q + 1) * S] = stage[n, pl.ds(q, OWN, stride=C), :]
+    for c in range(C):
+        weight_ref[pl.ds(c, C, stride=C), :] = gw_ref[c * C:(c + 1) * C, :]
+    bias_ref[...] = gb_ref[:1, :]
+    for c in save:
+        c.wait()
+
 def kernel(
     a_ref, b_ref, w_ref, bias_ref, cot_hbm,
     pair_hbm, gl_ref, gr_ref, gw_ref, gb_ref,
     cot, d, p, a_all, a_t, b_in, b_all, w_t, pair,
-    l_out, l_in, l_x, l_xin, r_keep, r_x, r_xin, r_out, r_in,
-    w0, w0_in, w1_out, w1_in, w2_out, w2_in, w3_out, w3_in, w5,
+    l_out, l_in, r_keep, r_x, r_xin, r_out, r_in,
+    w0, w0_in, w1_out, w1_in, w2_out, w_all,
     cot_sem, pair_sem, ax_s, ax_r, az_s, az_r, bc_s, bc_r, bx_s, bx_r, by_s, by_r,
-    l_s, l_r, lx_s, lx_r, rx_s, rx_r, r_s, r_r,
-    w0_s, w0_r, w1_s, w1_r, w2_s, w2_r, w3_s, w3_r, w4_s, w4_r, w5_s, w5_r,
+    l_s, l_r, rx_s, rx_r, r_s, r_r,
+    w0_s, w0_r, w1_s, w1_r, w2_s, w2_r, w3_s, w3_r,
 ):
     row = lax.axis_index("row")
     col = lax.axis_index("col")
@@ -47,6 +111,7 @@
     near = (1 - half) * 8 + y * 2 + core
     other = z * 2 + (1 - far)
     spot = half * 4 + y
+    chip = spot * COLS + col
 
     def row_y(n, h=None):
         return (half if h is None else h) * 8 + lax.rem(y + n + 4, 4) * 2 + core
@@ -57,6 +122,10 @@
     def row_spot(n):
         q = lax.rem(spot + n + 8, 8)
         return q, q * 2 + core
+
+    def chip_at(n):
+        m = lax.rem(chip + n + CHIPS, CHIPS)
+        return m, lax.div(m, COLS) * 2 + core, lax.rem(m, COLS)
 
     def send(src, dst, ss, rs, k, r=None, c=None):
         return pltpu.make_async_remote_copy(
@@ -83,13 +152,13 @@
 
     barrier = pltpu.get_barrier_semaphore()
 
-    def greet(r, c):
+    def greet(k):
+        _, r, c = chip_at(k + 1)
         pl.semaphore_signal(barrier, inc=1, device_id=(r, c), device_id_type=MESH)
 
-    each(COLS - 1, lambda k: greet(row, lax.rem(col + k + 1, COLS)))
-    each(7, lambda k: greet(row_spot(k + 1)[1], col))
-    greet(mate, col)
-    pl.semaphore_wait(barrier, 15)
+    each(CHIPS - 1, greet)
+    pl.semaphore_signal(barrier, inc=1, device_id=(mate, col), device_id_type=MESH)
+    pl.semaphore_wait(barrier, CHIPS)
 
     bx = send(b_ref, b_in.at[row], bx_s, bx_r, 0, r=near)
     bx.start()
@@ -159,13 +228,10 @@
         each(6, lambda k: send(b_ref, b_in.at[row], by_s, by_r, k, r=near).wait_send())
 
     gb_ref[...] = jnp.zeros_like(gb_ref)
-    group = 8
+    group = 16
 
     def d_step(g, carry):
-        @pl.when(lax.rem(g, 2) == 0)
-        def _():
-            cot_copy(lax.div(g, 2)).wait()
-
+        cot_copy(g).wait()
         block = cot[pl.ds(g * group, group)].reshape(group * TJ, CZ)
         r = dot(w_ref[...], block, NT).astype(BF16)
         for q in range(group):
@@ -175,9 +241,8 @@
 
     lax.fori_loop(0, 3, d_step, 0)
     relay_x()
-    lax.fori_loop(3, 6, d_step, 0)
+    lax.fori_loop(3, 4, d_step, 0)
     relay_y(half, 2, 0)
-    lax.fori_loop(6, 8, d_step, 0)
     end_a()
     for q in range(COLS):
         a_t[:, q * 256:(q + 1) * 256] = a_all[q].T
@@ -250,50 +315,47 @@
     w0_copy = send(w0.at[1 - core], w0_in, w0_s, w0_r, 0, r=mate)
     w0_copy.start()
 
+    def send_l(k, c, slot):
+        return send(l_out.at[c], l_in.at[slot], l_s, l_r, k, c=c)
+
     def gl_step(m, carry):
-        x = jnp.concatenate([d[q, pl.ds(m * 1024, 1024), :] for q in range(C)], axis=1)
+        to = lax.rem(z + 1 + m, 4)
+        x = jnp.concatenate([d[q, pl.ds(to * 512, 512), :] for q in range(C)], axis=1)
         r = (dot(x, b_all[...]) * (1.0 / S)).astype(BF16)
-        for h in range(4):
-            l_out[m * 4 + h] = r[h * 256:(h + 1) * 256, :]
+        for h in range(2):
+            l_out[to * 2 + h] = r[h * 256:(h + 1) * 256, :]
+        send_l(m * 2, to * 2 + far, col).start()
+        send_l(m * 2 + 1, to * 2 + 1 - far, col).start()
         return carry
 
     lax.fori_loop(0, 1, gl_step, 0)
 
     w0_copy.wait()
-    for q in range(COLS):
-        part = slice(q * 64, q * 64 + 64)
-        w1_out[q, :64, :] = w0[core, part, :] + w0_in[part, :]
-        w1_out[q, 64:, :] = w0[core, 512:, :] + w0_in[512:, :]
-
-    def send_w1(k, slot):
-        to = lax.rem(col + k + 1, COLS)
-        return send(w1_out.at[to], w1_in.at[slot], w1_s, w1_r, k, c=to)
-
-    each(COLS - 1, lambda k: send_w1(k, col).start())
-    w1_in[col] = w1_out[col]
-
-    lax.fori_loop(1, 2, gl_step, 0)
-
-    def send_l(k):
-        to = lax.rem(z + k + 1, 4)
-        return send(l_out.at[pl.ds(to * 2, 2)], l_in.at[k], l_s, l_r, k, c=to * 2 + far)
-
-    each(3, lambda k: send_l(k).start())
-
-    each(COLS - 1, lambda k: send_w1(k, lax.rem(col + COLS - 1 - k, COLS)).wait())
-    s1 = w1_in[0]
-    for q in range(1, COLS):
-        s1 += w1_in[q]
-    for q in range(8):
-        w2_out[q, :8, :] = s1[q * 8:(q + 1) * 8, :]
-        w2_out[q, 8:, :] = s1[64:, :]
-
-    def send_w2(k, slot):
-        q, r = row_spot(k + 1)
-        return send(w2_out.at[q], w2_in.at[slot], w2_s, w2_r, k, r=r)
-
-    each(7, lambda k: send_w2(k, spot).start())
-    w2_in[spot] = w2_out[spot]
+    v = (w0[core, :512, :] + w0_in[:512, :]).reshape(CHIPS, 8, CZ)
+    bias = jnp.sum(w0[core, 512:, :] + w0_in[512:, :], axis=0, keepdims=True)
+    upper = bias.astype(BF16).astype(F32)
+    place = lax.broadcasted_iota(jnp.int32, (8, CZ), 0)
+    extra = jnp.where(place == 0, upper, jnp.where(place == 1, bias - upper, 0.0))
+    w1_out[...] = jnp.concatenate([v, jnp.broadcast_to(extra, (CHIPS, 8, CZ))], axis=1).astype(BF16)
+
+    def send_w1(k):
+        m, r, c = chip_at(k + 1)
+        return send(w1_out.at[m], w1_in.at[chip], w1_s, w1_r, k, r=r, c=c)
+
+    each(CHIPS - 1, lambda k: send_w1(k).start())
+    w1_in[chip] = w1_out[chip]
+
+    lax.fori_loop(1, 3, gl_step, 0)
+
+    def gl_last():
+        x = jnp.concatenate([d[q, pl.ds(z * 512, 512), :] for q in range(C)], axis=1)
+        r = (dot(x, b_all[...]) * (1.0 / S)).astype(BF16)
+        for h in range(2):
+            l_out[z * 2 + h] = r[h * 256:(h + 1) * 256, :]
+        send_l(6, z * 2 + 1 - far, col).start()
+        l_in[col] = l_out[col]
+
+    gl_last()
 
     def pair_step(g, carry):
         x = jnp.concatenate(
@@ -307,41 +369,25 @@
 
     lax.fori_loop(0, 1, pair_step, 0)
 
-    each(7, lambda k: send_w2(k, row_spot(-1 - k)[0]).wait())
-    s2 = w2_in[0]
-    for q in range(1, 8):
-        s2 += w2_in[q]
-    w3_out[...] = s2[:8, :]
-    gb_ref[...] = s2[8:, :]
-
-    def send_w3(k, slot):
-        return send(w3_out, w3_in.at[slot], w3_s, w3_r, k, r=row_spot(k + 1)[1])
-
-    each(7, lambda k: send_w3(k, spot).start())
-    w3_in[spot] = w3_out[...]
-
-    lax.fori_loop(1, 2, pair_step, 0)
-
-    each(3, lambda k: send_l(k).wait())
-    mine = l_out[pl.ds(z * 2 + far, 1)][0].astype(F32)
-    theirs = l_out[pl.ds(z * 2 + 1 - far, 1)][0].astype(F32)
-    for k in range(3):
-        mine += l_in[k, far].astype(F32)
-        theirs += l_in[k, 1 - far].astype(F32)
-    l_x[...] = theirs.astype(BF16)
-    lx = send(l_x, l_xin, lx_s, lx_r, 0, c=other)
-    lx.start()
-    gl_ref[...] = mine
-
-    each(7, lambda k: send_w3(k, row_spot(-1 - k)[0]).wait())
-
-    def send_w4(k, slot):
-        return send(w3_in, w5.at[core, slot], w4_s, w4_r, k, c=lax.rem(col + k + 1, COLS))
-
-    each(COLS - 1, lambda k: send_w4(k, col).start())
-    w5[core, col] = w3_in[...]
-
-    lax.fori_loop(2, 4, pair_step, 0)
+    def wait_w1(k):
+        m, r, c = chip_at(k + 1)
+        send(w1_out.at[m], w1_in.at[chip_at(-1 - k)[0]], w1_s, w1_r, k, r=r, c=c).wait()
+
+    each(CHIPS - 1, wait_w1)
+    s1 = w1_in[0].astype(F32)
+    for q in range(1, CHIPS):
+        s1 += w1_in[q].astype(F32)
+    w2_out[...] = s1[:8, :]
+    gb_ref[...] = jnp.broadcast_to(s1[8:9, :] + s1[9:10, :], (8, CZ))
+
+    def send_w2(k, slot):
+        _, r, c = chip_at(k + 1)
+        return send(w2_out, w_all.at[core, slot], w2_s, w2_r, k, r=r, c=c)
+
+    each(CHIPS - 1, lambda k: send_w2(k, chip).start())
+    w_all[core, chip] = w2_out[...]
+
+    lax.fori_loop(1, 4, pair_step, 0)
 
     each(7, lambda k: send(r_out.at[0], r_in.at[row_spot(-1 - k)[0]], r_s, r_r, k, r=near).wait())
     total = r_in[0].astype(F32)
@@ -349,23 +395,42 @@
         total += r_in[q].astype(F32)
     gr_ref[...] = total
 
-    each(COLS - 1, lambda k: send_w4(k, lax.rem(col + COLS - 1 - k, COLS)).wait())
-    send(w5.at[core], w5.at[core], w5_s, w5_r, 0, r=mate).start()
-    lx.wait()
-    gl_ref[...] += l_xin[...].astype(F32)
-    send(w5.at[core], w5.at[1 - core], w5_s, w5_r, 0, r=mate).wait()
-    gw_ref[...] = w5[...].reshape(C * C, CZ)
+    def wait_l(k):
+        to = lax.rem(z + 1 + k, 4) * 2
+        of = lax.rem(z + 3 - k, 4) * 2
+        send_l(k * 2, to + far, of + far).wait()
+        send_l(k * 2 + 1, to + 1 - far, of + 1 - far).wait()
+
+    each(3, wait_l)
+    send_l(6, other, other).wait()
+    total = l_in[0].astype(F32)
+    for q in range(1, COLS):
+        total += l_in[q].astype(F32)
+    gl_ref[...] = total
+
+    each(CHIPS - 1, lambda k: send_w2(k, chip_at(-1 - k)[0]).wait())
+    send(w_all.at[core], w_all.at[core], w3_s, w3_r, 0, r=mate).start()
+    gw_ref[pl.ds(core * 512, 512), :] = w_all[core].reshape(512, CZ)
+    send(w_all.at[core], w_all.at[1 - core], w3_s, w3_r, 0, r=mate).wait()
+    gw_ref[pl.ds((1 - core) * 512, 512), :] = w_all[1 - core].reshape(512, CZ)
     each(4, lambda q: pair_copy(q).wait())
 
 
 def per_device(left_proj, right_proj, out_weight, out_bias, pair_cotangent):
-    a = (left_proj * BF16(1.0 / S)).reshape(OWN, S, C).transpose(0, 2, 1).reshape(OWN * C, S)
-    b = right_proj.reshape(OWN, S, C).transpose(2, 0, 1).reshape(C * OWN, S)
-    w = out_weight.reshape(C, C, CZ).transpose(1, 0, 2).reshape(C * C, CZ)
     vmem = pl.BlockSpec(memory_space=pltpu.VMEM)
     hbm = pl.BlockSpec(memory_space=pl.ANY)
     dma = pltpu.SemaphoreType.DMA
     own = OWN * C
+    a, b, w = pl.pallas_call(
+        prepare,
+        out_shape=(
+            jax.ShapeDtypeStruct((own, S), BF16),
+            jax.ShapeDtypeStruct((own, S), BF16),
+            jax.ShapeDtypeStruct((C * C, CZ), BF16),
+        ),
+        scratch_shapes=[pltpu.VMEM((2, own, S), F32), pltpu.VMEM((C * C, CZ), F32)],
+        name="prepare",
+    )(left_proj, right_proj, out_weight)
     pair, gl, gr, gw, gb = pl.pallas_call(
         kernel,
         out_shape=(
@@ -388,9 +453,7 @@
             pltpu.VMEM((CZ, C * C), BF16),
             pltpu.VMEM((TI, TJ, CZ), BF16),
             pltpu.VMEM((COLS, own, S), BF16),
-            pltpu.VMEM((3, 2, own, S), BF16),
-            pltpu.VMEM((own, S), BF16),
-            pltpu.VMEM((own, S), BF16),
+            pltpu.VMEM((COLS, own, S), BF16),
             pltpu.VMEM((8, own, S), F32),
             pltpu.VMEM((8, own, S), BF16),
             pltpu.VMEM((8, own, S), BF16),
@@ -398,30 +461,40 @@
             pltpu.VMEM((8, own, S), BF16),
             pltpu.VMEM((2, 520, CZ), F32),
             pltpu.VMEM((520, CZ), F32),
-            pltpu.VMEM((COLS, 72, CZ), F32),
-            pltpu.VMEM((COLS, 72, CZ), F32),
-            pltpu.VMEM((8, 16, CZ), F32),
-            pltpu.VMEM((8, 16, CZ), F32),
+            pltpu.VMEM((CHIPS, 16, CZ), BF16),
+            pltpu.VMEM((CHIPS, 16, CZ), BF16),
             pltpu.VMEM((8, CZ), F32),
-            pltpu.VMEM((8, 8, CZ), F32),
-            pltpu.VMEM((2, COLS, 8, 8, CZ), F32),
+            pltpu.VMEM((2, CHIPS, 8, CZ), F32),
             dma((4,)), dma((4,)),
             dma((1,)), dma((1,)), dma((6,)), dma((6,)),
             dma((8,)), dma((8,)), dma((1,)), dma((1,)), dma((6,)), dma((6,)),
-            dma((3,)), dma((3,)), dma((1,)), dma((1,)),
+            dma((7,)), dma((7,)),
             dma((4,)), dma((4,)), dma((7,)), dma((7,)),
-            dma((1,)), dma((1,)), dma((7,)), dma((7,)), dma((7,)), dma((7,)),
-            dma((7,)), dma((7,)), dma((7,)), dma((7,)), dma((1,)), dma((1,)),
+            dma((1,)), dma((1,)), dma((CHIPS - 1,)), dma((CHIPS - 1,)),
+            dma((CHIPS - 1,)), dma((CHIPS - 1,)), dma((1,)), dma((1,)),
         ],
         compiler_params=pltpu.CompilerParams(
             collective_id=0, has_side_effects=True, vmem_limit_bytes=60 << 20
         ),
         name="outer_product_mean",
     )(a, b, w, out_bias.reshape(1, CZ), pair_cotangent)
-    grad_left = gl.reshape(OWN, C, S).transpose(0, 2, 1).reshape(OWN, S * C)
-    grad_right = gr.reshape(C, OWN, S).transpose(1, 2, 0).reshape(OWN, S * C)
-    grad_weight = gw.reshape(C, C, CZ).transpose(1, 0, 2).reshape(C * C, CZ)
-    return pair, grad_left, grad_right, grad_weight, jnp.sum(gb, axis=0)
+    grad_left, grad_right, grad_weight, grad_bias, pair = pl.pallas_call(
+        finish,
+        out_shape=(
+            jax.ShapeDtypeStruct((OWN, S * C), F32),
+            jax.ShapeDtypeStruct((OWN, S * C), F32),
+            jax.ShapeDtypeStruct((C * C, CZ), F32),
+            jax.ShapeDtypeStruct((1, CZ), F32),
+            jax.ShapeDtypeStruct((TI, TJ, CZ), BF16),
+        ),
+        in_specs=[vmem, vmem, vmem, vmem, hbm],
+        out_specs=(vmem, vmem, vmem, vmem, hbm),
+        scratch_shapes=[
+            pltpu.VMEM((TI, TJ, CZ), BF16), pltpu.VMEM((2, own, S), F32), dma((4,)), dma((4,)),
+        ],
+        name="finish",
+    )(gl, gr, gw, gb, pair)
+    return pair, grad_left, grad_right, grad_weight, grad_bias.reshape(CZ)
 
 
 def solution(mesh):

time: 74.3 us -> 67.4 us (0.907)
  local copies, waits for them, and re-layouts: 10.9 us -> 0 us
  Pallas kernels: 60.2 us -> 66.4 us
  other arithmetic: 2.2 us -> 0 us
    reshape x7 -> x0, local copies, waits for them, and re-layouts: 6.99 us -> none  [the longest x2 1.99 us: per_device(): grad_right = gr.reshape(C, OWN, S).transpose(1, 2, 0).reshape(OWN, S * C)]
    pallas_call x0 -> x2, Pallas kernels: none -> 6.94 us  [the longest x1 4.49 us: per_device(): pl.pallas_call(finish, out_shape=(jax.ShapeDtypeStruct((OWN, S * C), F32)...]
    transpose x3 -> x0, local copies, waits for them, and re-layouts: 2.61 us -> none  [the longest x1 1.1 us: per_device(): grad_weight = gw.reshape(C, C, CZ).transpose(1, 0, 2).reshape(C * C, CZ)]
    reduce_sum x1 -> x0, other arithmetic: 1.36 us -> none  [per_device(): return (pair, grad_left, grad_right, grad_weight, jnp.sum(gb, axis=0))]
    unnamed x5 -> x0, local copies, waits for them, and re-layouts: 1.33 us -> none
    mul x1 -> x0, other arithmetic: 0.85 us -> none  [per_device(): left_proj * BF16(1.0 / S)]
    pallas_call x1, Pallas kernels: 60.2 us -> 59.4 us  [per_device(): pl.pallas_call(kernel, out_shape=(jax.ShapeDtypeStruct((TI, TJ, CZ), BF16...]
where the time goes in v3:
time: 67.4 us; the launch traced here: 67.2 us
  Pallas kernels  66.4 us (99%)
  between operations  0.8 us (1%)
    pallas_call x1, Pallas kernels, per_device(): pl.pallas_call(kernel, out_shape=(jax.ShapeDtypeStruct((TI, TJ, CZ), BF16...  59.4 us
    pallas_call x1, Pallas kernels, per_device(): pl.pallas_call(finish, out_shape=(jax.ShapeDtypeStruct((OWN, S * C), F32)...  4.49 us
    pallas_call x1, Pallas kernels, per_device(): pl.pallas_call(prepare, out_shape=(jax.ShapeDtypeStruct((own, S), BF16),...  2.46 us

profile of v3, /device:TPU:1, one launch (start us, length us, event | category | flops | bytes accessed | tf_op | source)
XLA Modules:
  0.0 67.2 jit_solution(5444597494357020767)
XLA Ops:
  0.6 2.5 %prepare.1 = (bf16[256,128]{1,0:T(8,128)(2,1)}, bf16[256,128]{1,0:T(8,128)(2,1)}, bf16[1024,128]{1,0:T(8,128)(2,1)}) custom-call(bf16[8,4096]{1,0:T(8,128)(2,1)} %left_ref.1, bf16[8,4096]{1,0:T(8,128)(2,1)} %right_ref.1, bf16[1024,128]{1,0:T(8,128)(2,1)} %weight_ref.1), custom_call_target="tpu_custom_call" | custom-call | tf_op jit(solution)/shard_map/prepare/pallas_call | solution.py:424
  3.1 59.4 %outer_product_mean.1 = (bf16[64,128,128]{2,1,0:T(8,128)(2,1)}, f32[256,128]{1,0:T(8,128)}, f32[256,128]{1,0:T(8,128)}, f32[1024,128]{1,0:T(8,128)}, f32[8,128]{1,0:T(8,128)}) custom-call(bf16[256,128]{1,0:T(8,128)(2,1)} %get-tuple-element.18.a_ref, bf16[256,128]{1,0:T(8,128)(2,1)} %get-tuple-element.19.b_ref, bf16[1024,128]{1,0:T(8,128)(2,1)} %get-tuple-element.20.w_ref, ...), custom_call_target="tpu_custom_call" | custom-call | tf_op jit(solution)/shard_map/outer_product_mean/pallas_call | solution.py:434
  62.5 4.5 %finish.1 = (f32[8,4096]{1,0:T(8,128)}, f32[8,4096]{1,0:T(8,128)}, f32[1024,128]{1,0:T(8,128)}, f32[1,128]{1,0:T(1,128)}, bf16[64,128,128]{2,1,0:T(8,128)(2,1)}) custom-call(f32[256,128]{1,0:T(8,128)} %get-tuple-element.21.gl_ref, f32[256,128]{1,0:T(8,128)} %get-tuple-element.22.gr_ref, f32[1024,128]{1,0:T(8,128)} %get-tuple-element.23.gw_ref, ...), custom_call_target="tpu_custom_call" | custom-call | tf_op jit(solution)/shard_map/finish/pallas_call | solution.py:481

commit v4 on v3

--- a/solution.py
+++ b/solution.py
@@ -39,61 +39,19 @@
     return out
 
 
-def prepare(left_ref, right_ref, weight_ref, a_ref, b_ref, w_ref, stage, flat):
-    for n, ref in enumerate((left_ref, right_ref)):
-        for q in range(C):
-            stage[n, q * OWN:(q + 1) * OWN, :] = ref[:, q * S:(q + 1) * S].astype(F32)
-    for n in range(2):
-        for g in range(2):
-            x = jnp.concatenate([stage[n, pl.ds(g * 4 + i, C, stride=OWN), :] for i in range(4)], axis=0)
-            t = x.T
-            parts = swap([t[m * C:(m + 1) * C] for m in range(4)])
-            for i in range(4):
-                if n == 0:
-                    a_ref[(g * 4 + i) * C:(g * 4 + i + 1) * C, :] = (parts[i] * (1.0 / S)).astype(BF16)
-                else:
-                    flat[pl.ds(g * 4 + i, C, stride=OWN), :] = parts[i]
-    b_ref[...] = flat[:OWN * C, :].astype(BF16)
-    flat[...] = weight_ref[...].astype(F32)
-    for c in range(C):
-        w_ref[c * C:(c + 1) * C, :] = flat[pl.ds(c, C, stride=C), :].astype(BF16)
-
-
-def finish(
-    gl_ref, gr_ref, gw_ref, gb_ref, pair_in,
-    left_ref, right_ref, weight_ref, bias_ref, pair_out, hold, stage, in_sem, out_sem,
-):
-    def part(ref, q):
-        return ref.at[pl.ds(q * 16, 16)]
-
-    load = [pltpu.make_async_copy(part(pair_in, q), part(hold, q), in_sem.at[q]) for q in range(4)]
-    save = [pltpu.make_async_copy(part(hold, q), part(pair_out, q), out_sem.at[q]) for q in range(4)]
-    for c in load:
+def finish(*refs):
+    ins, outs, sem = refs[:5], refs[5:10], refs[10]
+    copies = [pltpu.make_async_copy(ins[q], outs[q], sem.at[q]) for q in range(5)]
+    for c in copies:
         c.start()
-    for n, (ref, out) in enumerate(((gl_ref, left_ref), (gr_ref, right_ref))):
-        for g in range(2):
-            rows = [
-                ref[(g * 4 + i) * C:(g * 4 + i + 1) * C, :] if n == 0
-                else ref[pl.ds(g * 4 + i, C, stride=OWN), :]
-                for i in range(4)
-            ]
-            stage[n, g * S:(g + 1) * S, :] = jnp.concatenate(swap(rows), axis=0).T
-    for q in range(4):
-        load[q].wait()
-        save[q].start()
-    for n, out in enumerate((left_ref, right_ref)):
-        for q in range(C):
-            out[:, q * S:(q + 1) * S] = stage[n, pl.ds(q, OWN, stride=C), :]
-    for c in range(C):
-        weight_ref[pl.ds(c, C, stride=C), :] = gw_ref[c * C:(c + 1) * C, :]
-    bias_ref[...] = gb_ref[:1, :]
-    for c in save:
+    for c in copies:
         c.wait()
 
+
 def kernel(
-    a_ref, b_ref, w_ref, bias_ref, cot_hbm,
-    pair_hbm, gl_ref, gr_ref, gw_ref, gb_ref,
-    cot, d, p, a_all, a_t, b_in, b_all, w_t, pair,
+    left_ref, right_ref, weight_ref, bias_ref, cot_hbm,
+    pair_hbm, gl_ref, gr_ref, gw_ref, bsum_ref,
+    gb_ref, stage, flat, cot, d, p, a_all, a_t, b_in, b_all, w_ref, w_t, pair,
     l_out, l_in, r_keep, r_x, r_xin, r_out, r_in,
     w0, w0_in, w1_out, w1_in, w2_out, w_all,
     cot_sem, pair_sem, ax_s, ax_r, az_s, az_r, bc_s, bc_r, bx_s, bx_r, by_s, by_r,
@@ -152,13 +110,30 @@
 
     barrier = pltpu.get_barrier_semaphore()
 
-    def greet(k):
-        _, r, c = chip_at(k + 1)
+    def greet(r, c):
         pl.semaphore_signal(barrier, inc=1, device_id=(r, c), device_id_type=MESH)
 
-    each(CHIPS - 1, greet)
-    pl.semaphore_signal(barrier, inc=1, device_id=(mate, col), device_id_type=MESH)
-    pl.semaphore_wait(barrier, CHIPS)
+    each(COLS - 1, lambda k: greet(row, lax.rem(col + k + 1, COLS)))
+    each(7, lambda k: greet(row_spot(k + 1)[1], col))
+    greet(mate, col)
+
+    for n, ref in enumerate((left_ref, right_ref)):
+        for q in range(C):
+            stage[n, q * OWN:(q + 1) * OWN, :] = ref[:, q * S:(q + 1) * S].astype(F32)
+    for n in range(2):
+        for g in range(2):
+            x = jnp.concatenate([stage[n, pl.ds(g * 4 + i, C, stride=OWN), :] for i in range(4)], axis=0)
+            t = x.T
+            parts = swap([t[m * C:(m + 1) * C] for m in range(4)])
+            for i in range(4):
+                if n == 0:
+                    a_all[col, (g * 4 + i) * C:(g * 4 + i + 1) * C, :] = (parts[i] * (1.0 / S)).astype(BF16)
+                else:
+                    flat[pl.ds(g * 4 + i, C, stride=OWN), :] = parts[i]
+    b_in[row] = flat[:OWN * C, :].astype(BF16)
+    a_ref = a_all.at[col]
+    b_ref = b_in.at[row]
+    pl.semaphore_wait(barrier, 15)
 
     bx = send(b_ref, b_in.at[row], bx_s, bx_r, 0, r=near)
     bx.start()
@@ -188,8 +163,9 @@
     each(3, lambda k: by_own(k).start())
     each(3, lambda k: az_own(k).start())
     bc_own.start()
-    a_all[col] = a_ref[...]
-    b_in[row] = b_ref[...]
+    flat[...] = weight_ref[...].astype(F32)
+    for c in range(C):
+        w_ref[c * C:(c + 1) * C, :] = flat[pl.ds(c, C, stride=C), :].astype(BF16)
     w_t[...] = w_ref[...].T
 
     def relay_x():
@@ -243,10 +219,43 @@
     relay_x()
     lax.fori_loop(3, 4, d_step, 0)
     relay_y(half, 2, 0)
+    relay_y(1 - half, 5, 3)
     end_a()
+    end_b()
+
+    def lay_b(q, carry):
+        part = b_in[:, pl.ds(q * 16, 16), :].astype(F32)
+        for h in range(2):
+            b_all[pl.ds((q * 2 + h) * TJ, TJ), :] = part[:, h * 8:(h + 1) * 8, :].reshape(TJ, S).astype(BF16)
+        return carry
+
+    lax.fori_loop(0, C // 2, lay_b, 0, unroll=4)
+
+    def p_step(n, carry):
+        rhs = b_all[pl.ds(n * 2048, 2048), :]
+        for m in range(8):
+            r = dot(a_all[m], rhs, NT).astype(BF16)
+            for q in range(16):
+                p[n * 16 + q, m * 256:(m + 1) * 256, :] = r[:, q * TJ:(q + 1) * TJ]
+        return carry
+
+    lax.fori_loop(0, 2, p_step, 0)
+
+    def gw_step(g, carry):
+        x = jnp.concatenate(
+            [p[pl.ds(g * 16, 16), q * C:(q + 1) * C, :].reshape(16 * C, TJ) for q in range(TI)], axis=1
+        )
+        w0[g, :512, :] = dot(x, cot[...].reshape(TI * TJ, CZ))
+        return carry
+
+    lax.fori_loop(0, 2, gw_step, 0)
+    w0[0, 512:, :] = gb_ref[...]
+    w0[1, 512:, :] = gb_ref[...]
+    w0_copy = send(w0.at[1 - core], w0_in, w0_s, w0_r, 0, r=mate)
+    w0_copy.start()
+
     for q in range(COLS):
         a_t[:, q * 256:(q + 1) * 256] = a_all[q].T
-    relay_y(1 - half, 5, 3)
 
     def rx(g):
         part = pl.ds(g * 64, 64)
@@ -265,55 +274,24 @@
         rx(g).start()
         return carry
 
-    lax.fori_loop(0, C // 8, gr_step, 0)
-
-    end_b()
-
-    def lay_b(q, carry):
-        part = b_in[:, pl.ds(q * 16, 16), :].astype(F32)
-        for h in range(2):
-            b_all[pl.ds((q * 2 + h) * TJ, TJ), :] = part[:, h * 8:(h + 1) * 8, :].reshape(TJ, S).astype(BF16)
-        return carry
-
-    lax.fori_loop(0, C // 2, lay_b, 0, unroll=4)
-
-    def p_step(n, carry):
-        rhs = b_all[pl.ds(n * 2048, 2048), :]
-        for m in range(8):
-            r = dot(a_all[m], rhs, NT).astype(BF16)
-            for q in range(16):
-                p[n * 16 + q, m * 256:(m + 1) * 256, :] = r[:, q * TJ:(q + 1) * TJ]
-        return carry
-
-    lax.fori_loop(0, 1, p_step, 0)
-
-    def send_r(k):
-        q, r = row_spot(k + 1)
-        return send(r_out.at[q], r_in.at[spot], r_s, r_r, k, r=r)
-
-    each(4, lambda g: rx(g).wait())
-
-    def sum_x(q):
-        r_out[q] = (r_keep[q] + r_xin[q].astype(F32)).astype(BF16)
-
-    each(8, sum_x)
-    each(7, lambda k: send_r(k).start())
-    r_in[spot] = r_out[spot]
-
-    lax.fori_loop(1, 2, p_step, 0)
-
-    def gw_step(g, carry):
-        x = jnp.concatenate(
-            [p[pl.ds(g * 16, 16), q * C:(q + 1) * C, :].reshape(16 * C, TJ) for q in range(TI)], axis=1
-        )
-        w0[g, :512, :] = dot(x, cot[...].reshape(TI * TJ, CZ))
-        return carry
-
-    lax.fori_loop(0, 2, gw_step, 0)
-    w0[0, 512:, :] = gb_ref[...]
-    w0[1, 512:, :] = gb_ref[...]
-    w0_copy = send(w0.at[1 - core], w0_in, w0_s, w0_r, 0, r=mate)
-    w0_copy.start()
+    lax.fori_loop(0, 1, gr_step, 0)
+
+    w0_copy.wait()
+    v = (w0[core, :512, :] + w0_in[:512, :]).reshape(CHIPS, 8, CZ)
+    bias = jnp.sum(w0[core, 512:, :] + w0_in[512:, :], axis=0, keepdims=True)
+    upper = bias.astype(BF16).astype(F32)
+    place = lax.broadcasted_iota(jnp.int32, (8, CZ), 0)
+    extra = jnp.where(place == 0, upper, jnp.where(place == 1, bias - upper, 0.0))
+    w1_out[...] = jnp.concatenate([v, jnp.broadcast_to(extra, (CHIPS, 8, CZ))], axis=1).astype(BF16)
+
+    def send_w1(k):
+        m, r, c = chip_at(k + 1)
+        return send(w1_out.at[m], w1_in.at[chip], w1_s, w1_r, k, r=r, c=c)
+
+    each(CHIPS - 1, lambda k: send_w1(k).start())
+    w1_in[chip] = w1_out[chip]
+
+    lax.fori_loop(1, 4, gr_step, 0)
 
     def send_l(k, c, slot):
         return send(l_out.at[c], l_in.at[slot], l_s, l_r, k, c=c)
@@ -330,20 +308,18 @@
 
     lax.fori_loop(0, 1, gl_step, 0)
 
-    w0_copy.wait()
-    v = (w0[core, :512, :] + w0_in[:512, :]).reshape(CHIPS, 8, CZ)
-    bias = jnp.sum(w0[core, 512:, :] + w0_in[512:, :], axis=0, keepdims=True)
-    upper = bias.astype(BF16).astype(F32)
-    place = lax.broadcasted_iota(jnp.int32, (8, CZ), 0)
-    extra = jnp.where(place == 0, upper, jnp.where(place == 1, bias - upper, 0.0))
-    w1_out[...] = jnp.concatenate([v, jnp.broadcast_to(extra, (CHIPS, 8, CZ))], axis=1).astype(BF16)
-
-    def send_w1(k):
-        m, r, c = chip_at(k + 1)
-        return send(w1_out.at[m], w1_in.at[chip], w1_s, w1_r, k, r=r, c=c)
-
-    each(CHIPS - 1, lambda k: send_w1(k).start())
-    w1_in[chip] = w1_out[chip]
+    def send_r(k):
+        q, r = row_spot(k + 1)
+        return send(r_out.at[q], r_in.at[spot], r_s, r_r, k, r=r)
+
+    each(4, lambda g: rx(g).wait())
+
+    def sum_x(q):
+        r_out[q] = (r_keep[q] + r_xin[q].astype(F32)).astype(BF16)
+
+    each(8, sum_x)
+    each(7, lambda k: send_r(k).start())
+    r_in[spot] = r_out[spot]
 
     lax.fori_loop(1, 3, gl_step, 0)
 
@@ -367,7 +343,7 @@
         pair_copy(g).start()
         return carry
 
-    lax.fori_loop(0, 1, pair_step, 0)
+    lax.fori_loop(0, 2, pair_step, 0)
 
     def wait_w1(k):
         m, r, c = chip_at(k + 1)
@@ -378,7 +354,7 @@
     for q in range(1, CHIPS):
         s1 += w1_in[q].astype(F32)
     w2_out[...] = s1[:8, :]
-    gb_ref[...] = jnp.broadcast_to(s1[8:9, :] + s1[9:10, :], (8, CZ))
+    bsum_ref[...] = s1[8:9, :] + s1[9:10, :]
 
     def send_w2(k, slot):
         _, r, c = chip_at(k + 1)
@@ -387,13 +363,20 @@
     each(CHIPS - 1, lambda k: send_w2(k, chip).start())
     w_all[core, chip] = w2_out[...]
 
-    lax.fori_loop(1, 4, pair_step, 0)
+    lax.fori_loop(2, 4, pair_step, 0)
+
+    def lay_out(n, rows, out):
+        for g in range(2):
+            stage[n, g * S:(g + 1) * S, :] = jnp.concatenate(swap(rows[g * 4:g * 4 + 4]), axis=0).T
+        for q in range(C):
+            out[:, q * S:(q + 1) * S] = stage[n, pl.ds(q, OWN, stride=C), :]
 
     each(7, lambda k: send(r_out.at[0], r_in.at[row_spot(-1 - k)[0]], r_s, r_r, k, r=near).wait())
     total = r_in[0].astype(F32)
     for q in range(1, 8):
         total += r_in[q].astype(F32)
-    gr_ref[...] = total
+    flat[:OWN * C, :] = total
+    lay_out(1, [flat[pl.ds(i, C, stride=OWN), :] for i in range(OWN)], gr_ref)
 
     def wait_l(k):
         to = lax.rem(z + 1 + k, 4) * 2
@@ -406,13 +389,13 @@
     total = l_in[0].astype(F32)
     for q in range(1, COLS):
         total += l_in[q].astype(F32)
-    gl_ref[...] = total
+    lay_out(0, [total[i * C:(i + 1) * C, :] for i in range(OWN)], gl_ref)
 
     each(CHIPS - 1, lambda k: send_w2(k, chip_at(-1 - k)[0]).wait())
     send(w_all.at[core], w_all.at[core], w3_s, w3_r, 0, r=mate).start()
-    gw_ref[pl.ds(core * 512, 512), :] = w_all[core].reshape(512, CZ)
     send(w_all.at[core], w_all.at[1 - core], w3_s, w3_r, 0, r=mate).wait()
-    gw_ref[pl.ds((1 - core) * 512, 512), :] = w_all[1 - core].reshape(512, CZ)
+    for c in range(C):
+        gw_ref[pl.ds(c, C, stride=C), :] = w_all[c // 16, c % 16 * 4:c % 16 * 4 + 4].reshape(C, CZ)
     each(4, lambda q: pair_copy(q).wait())
 
 
@@ -421,28 +404,21 @@
     hbm = pl.BlockSpec(memory_space=pl.ANY)
     dma = pltpu.SemaphoreType.DMA
     own = OWN * C
-    a, b, w = pl.pallas_call(
-        prepare,
-        out_shape=(
-            jax.ShapeDtypeStruct((own, S), BF16),
-            jax.ShapeDtypeStruct((own, S), BF16),
-            jax.ShapeDtypeStruct((C * C, CZ), BF16),
-        ),
-        scratch_shapes=[pltpu.VMEM((2, own, S), F32), pltpu.VMEM((C * C, CZ), F32)],
-        name="prepare",
-    )(left_proj, right_proj, out_weight)
     pair, gl, gr, gw, gb = pl.pallas_call(
         kernel,
         out_shape=(
             jax.ShapeDtypeStruct((TI, TJ, CZ), BF16),
-            jax.ShapeDtypeStruct((own, S), F32),
-            jax.ShapeDtypeStruct((own, S), F32),
+            jax.ShapeDtypeStruct((OWN, S * C), F32),
+            jax.ShapeDtypeStruct((OWN, S * C), F32),
             jax.ShapeDtypeStruct((C * C, CZ), F32),
-            jax.ShapeDtypeStruct((8, CZ), F32),
+            jax.ShapeDtypeStruct((1, CZ), F32),
         ),
         in_specs=[vmem, vmem, vmem, vmem, hbm],
         out_specs=(hbm, vmem, vmem, vmem, vmem),
         scratch_shapes=[
+            pltpu.VMEM((8, CZ), F32),
+            pltpu.VMEM((2, own, S), F32),
+            pltpu.VMEM((C * C, CZ), F32),
             pltpu.VMEM((TI, TJ, CZ), BF16),
             pltpu.VMEM((C, TI * C, TJ), BF16),
             pltpu.VMEM((C, TI * C, TJ), BF16),
@@ -450,6 +426,7 @@
             pltpu.VMEM((S, TI * C), BF16),
             pltpu.VMEM((ROWS, own, S), BF16),
             pltpu.VMEM((C * TJ, S), BF16),
+            pltpu.VMEM((C * C, CZ), BF16),
             pltpu.VMEM((CZ, C * C), BF16),
             pltpu.VMEM((TI, TJ, CZ), BF16),
             pltpu.VMEM((COLS, own, S), BF16),
@@ -474,10 +451,10 @@
             dma((CHIPS - 1,)), dma((CHIPS - 1,)), dma((1,)), dma((1,)),
         ],
         compiler_params=pltpu.CompilerParams(
-            collective_id=0, has_side_effects=True, vmem_limit_bytes=60 << 20
+            collective_id=0, has_side_effects=True, vmem_limit_bytes=56 << 20
         ),
         name="outer_product_mean",
-    )(a, b, w, out_bias.reshape(1, CZ), pair_cotangent)
+    )(left_proj, right_proj, out_weight, out_bias.reshape(1, CZ), pair_cotangent)
     grad_left, grad_right, grad_weight, grad_bias, pair = pl.pallas_call(
         finish,
         out_shape=(
@@ -487,11 +464,9 @@
             jax.ShapeDtypeStruct((1, CZ), F32),
             jax.ShapeDtypeStruct((TI, TJ, CZ), BF16),
         ),
-        in_specs=[vmem, vmem, vmem, vmem, hbm],
-        out_specs=(vmem, vmem, vmem, vmem, hbm),
-        scratch_shapes=[
-            pltpu.VMEM((TI, TJ, CZ), BF16), pltpu.VMEM((2, own, S), F32), dma((4,)), dma((4,)),
-        ],
+        in_specs=[vmem] * 5,
+        out_specs=(hbm,) * 5,
+        scratch_shapes=[dma((5,))],
         name="finish",
     )(gl, gr, gw, gb, pair)
     return pair, grad_left, grad_right, grad_weight, grad_bias.reshape(CZ)

time: 67.4 us -> 66.4 us (0.985)
  Pallas kernels: 66.4 us -> 65.4 us
    pallas_call x1 -> x0, Pallas kernels: 2.46 us -> none  [per_device(): pl.pallas_call(prepare, out_shape=(jax.ShapeDtypeStruct((own, S), BF16),...]
    pallas_call x1, Pallas kernels: 59.4 us -> 61.9 us  [per_device(): pl.pallas_call(kernel, out_shape=(jax.ShapeDtypeStruct((TI, TJ, CZ), BF16...]
    pallas_call x1, Pallas kernels: 4.49 us -> 3.53 us  [per_device(): pl.pallas_call(finish, out_shape=(jax.ShapeDtypeStruct((OWN, S * C), F32)...]
where the time goes in v4:
time: 66.4 us; the launch traced here: 66.2 us
  Pallas kernels  65.4 us (98%)
  between operations  0.8 us (1%)
    pallas_call x1, Pallas kernels, per_device(): pl.pallas_call(kernel, out_shape=(jax.ShapeDtypeStruct((TI, TJ, CZ), BF16...  61.9 us
    pallas_call x1, Pallas kernels, per_device(): pl.pallas_call(finish, out_shape=(jax.ShapeDtypeStruct((OWN, S * C), F32)...  3.53 us

profile of v4, /device:TPU:1, one launch (start us, length us, event | category | flops | bytes accessed | tf_op | source)
XLA Modules:
  0.0 66.2 jit_solution(14997283274158858571)
XLA Ops:
  0.6 61.9 %outer_product_mean.1 = (bf16[64,128,128]{2,1,0:T(8,128)(2,1)}, f32[8,4096]{1,0:T(8,128)}, f32[8,4096]{1,0:T(8,128)}, f32[1024,128]{1,0:T(8,128)}, f32[1,128]{1,0:T(1,128)}) custom-call(bf16[8,4096]{1,0:T(8,128)(2,1)} %left_ref.1, bf16[8,4096]{1,0:T(8,128)(2,1)} %right_ref.1, bf16[1024,128]{1,0:T(8,128)(2,1)} %weight_ref.1, f32[1,128]{1,0:T(1,128)} %bitcast.2, ...), custom_call_target="tpu_custom_call" | custom-call | tf_op jit(solution)/shard_map/outer_product_mean/pallas_call | solution.py:407
  62.5 3.5 %finish.1 = (f32[8,4096]{1,0:T(8,128)}, f32[8,4096]{1,0:T(8,128)}, f32[1024,128]{1,0:T(8,128)}, f32[1,128]{1,0:T(1,128)}, bf16[64,128,128]{2,1,0:T(8,128)(2,1)}) custom-call(f32[8,4096]{1,0:T(8,128)} %get-tuple-element.15.refs_0_, f32[8,4096]{1,0:T(8,128)} %get-tuple-element.16.refs_1_, f32[1024,128]{1,0:T(8,128)} %get-tuple-element.17.refs_2_, ...), custom_call_target="tpu_custom_call" | custom-call | tf_op jit(solution)/shard_map/finish/pallas_call | solution.py:458

commit v5 on v4

--- a/solution.py
+++ b/solution.py
@@ -40,17 +40,28 @@
 
 
 def finish(*refs):
-    ins, outs, sem = refs[:5], refs[5:10], refs[10]
-    copies = [pltpu.make_async_copy(ins[q], outs[q], sem.at[q]) for q in range(5)]
-    for c in copies:
+    ins, outs, hold, sem = refs[:5], refs[5:10], refs[10:15], refs[15]
+    load, save = [], []
+    for q in range(5):
+        pieces = 4 if q == 4 else 1
+        for k in range(pieces):
+            n = ins[q].shape[0] // pieces
+            part = pl.ds(k * n, n)
+            load.append(pltpu.make_async_copy(ins[q].at[part], hold[q].at[part], sem.at[0, q + k]))
+            save.append(pltpu.make_async_copy(hold[q].at[part], outs[q].at[part], sem.at[1, q + k]))
+    for c in load:
         c.start()
-    for c in copies:
+    for c, e in zip(load, save):
         c.wait()
+        e.start()
+    for c in save:
+        c.wait()
 
 
 def kernel(
-    left_ref, right_ref, weight_ref, bias_ref, cot_hbm,
-    pair_hbm, gl_ref, gr_ref, gw_ref, bsum_ref,
+    left_hbm, right_hbm, weight_hbm, bias_ref, cot_hbm,
+    pair_hbm, gl_hbm, gr_hbm, gw_hbm, bsum_ref,
+    left_ref, right_ref, weight_ref, gl_ref, gr_ref, gw_ref, r_acc, in_sem, out_sem,
     gb_ref, stage, flat, cot, d, p, a_all, a_t, b_in, b_all, w_ref, w_t, pair,
     l_out, l_in, r_keep, r_x, r_xin, r_out, r_in,
     w0, w0_in, w1_out, w1_in, w2_out, w_all,
@@ -106,7 +117,14 @@
         part = pl.ds(q * 16, 16)
         return pltpu.make_async_copy(pair.at[part], pair_hbm.at[part], pair_sem.at[q])
 
-    each(4, lambda q: cot_copy(q).start())
+    own_in = [
+        pltpu.make_async_copy(src, dst, in_sem.at[q])
+        for q, (src, dst) in enumerate(
+            ((left_hbm, left_ref), (right_hbm, right_ref), (weight_hbm, weight_ref))
+        )
+    ]
+    for q in range(3):
+        own_in[q].start()
 
     barrier = pltpu.get_barrier_semaphore()
 
@@ -116,6 +134,10 @@
     each(COLS - 1, lambda k: greet(row, lax.rem(col + k + 1, COLS)))
     each(7, lambda k: greet(row_spot(k + 1)[1], col))
     greet(mate, col)
+
+    each(4, lambda q: cot_copy(q).start())
+    own_in[0].wait()
+    own_in[1].wait()
 
     for n, ref in enumerate((left_ref, right_ref)):
         for q in range(C):
@@ -163,6 +185,7 @@
     each(3, lambda k: by_own(k).start())
     each(3, lambda k: az_own(k).start())
     bc_own.start()
+    own_in[2].wait()
     flat[...] = weight_ref[...].astype(F32)
     for c in range(C):
         w_ref[c * C:(c + 1) * C, :] = flat[pl.ds(c, C, stride=C), :].astype(BF16)
@@ -183,13 +206,12 @@
 
         each(3, step)
 
-    def end_a():
+    def wait_a(near_part):
         def step(k):
-            send(a_ref, a_all.at[col_z(-1 - k)], az_s, az_r, k, c=col_z(k + 1)).wait()
-            send(a_ref, a_all.at[col_z(-1 - k, 1 - far)], az_s, az_r, k + 3, c=col_z(k + 1)).wait()
+            f, n = (far, 0) if near_part else (1 - far, 3)
+            send(a_ref, a_all.at[col_z(-1 - k, f)], az_s, az_r, k + n, c=col_z(k + 1)).wait()
 
         each(3, step)
-        ax.wait_send()
 
     def end_b():
         def from_mate(k, r):
@@ -218,52 +240,32 @@
     lax.fori_loop(0, 3, d_step, 0)
     relay_x()
     lax.fori_loop(3, 4, d_step, 0)
-    relay_y(half, 2, 0)
-    relay_y(1 - half, 5, 3)
-    end_a()
-    end_b()
-
-    def lay_b(q, carry):
-        part = b_in[:, pl.ds(q * 16, 16), :].astype(F32)
-        for h in range(2):
-            b_all[pl.ds((q * 2 + h) * TJ, TJ), :] = part[:, h * 8:(h + 1) * 8, :].reshape(TJ, S).astype(BF16)
-        return carry
-
-    lax.fori_loop(0, C // 2, lay_b, 0, unroll=4)
-
-    def p_step(n, carry):
-        rhs = b_all[pl.ds(n * 2048, 2048), :]
-        for m in range(8):
-            r = dot(a_all[m], rhs, NT).astype(BF16)
-            for q in range(16):
-                p[n * 16 + q, m * 256:(m + 1) * 256, :] = r[:, q * TJ:(q + 1) * TJ]
-        return carry
-
-    lax.fori_loop(0, 2, p_step, 0)
-
-    def gw_step(g, carry):
-        x = jnp.concatenate(
-            [p[pl.ds(g * 16, 16), q * C:(q + 1) * C, :].reshape(16 * C, TJ) for q in range(TI)], axis=1
-        )
-        w0[g, :512, :] = dot(x, cot[...].reshape(TI * TJ, CZ))
-        return carry
-
-    lax.fori_loop(0, 2, gw_step, 0)
-    w0[0, 512:, :] = gb_ref[...]
-    w0[1, 512:, :] = gb_ref[...]
-    w0_copy = send(w0.at[1 - core], w0_in, w0_s, w0_r, 0, r=mate)
-    w0_copy.start()
-
-    for q in range(COLS):
-        a_t[:, q * 256:(q + 1) * 256] = a_all[q].T
-
     def rx(g):
         part = pl.ds(g * 64, 64)
         return send(r_x.at[:, part], r_xin.at[:, part], rx_s, rx_r, g, r=mate)
 
+    def gr_part(g, f):
+        x = jnp.concatenate(
+            [
+                jnp.concatenate(
+                    [d[g * 8 + q, pl.ds((n * 2 + f) * 256, 256), :] for n in range(4)], axis=0
+                )
+                for q in range(8)
+            ],
+            axis=1,
+        )
+        return dot(a_t[...], x)
+
+    def lay_a(f):
+        for n in range(4):
+            a_t[:, n * 256:(n + 1) * 256] = a_all[n * 2 + f].T
+
+    def gr_first(g, carry):
+        r_acc[g] = gr_part(g, far)
+        return carry
+
     def gr_step(g, carry):
-        x = jnp.concatenate([d[g * 8 + q] for q in range(8)], axis=1)
-        r = dot(a_t[...], x)
+        r = r_acc[g] + gr_part(g, 1 - far)
         t = [r[:, q * TJ:(q + 1) * TJ].T.reshape(8, 16, S) for q in range(8)]
         even = [jnp.where(core == 0, v[:, :8], v[:, 8:]) for v in t]
         odd = [jnp.where(core == 0, v[:, 8:], v[:, :8]) for v in t]
@@ -274,24 +276,63 @@
         rx(g).start()
         return carry
 
-    lax.fori_loop(0, 1, gr_step, 0)
-
-    w0_copy.wait()
-    v = (w0[core, :512, :] + w0_in[:512, :]).reshape(CHIPS, 8, CZ)
-    bias = jnp.sum(w0[core, 512:, :] + w0_in[512:, :], axis=0, keepdims=True)
-    upper = bias.astype(BF16).astype(F32)
-    place = lax.broadcasted_iota(jnp.int32, (8, CZ), 0)
-    extra = jnp.where(place == 0, upper, jnp.where(place == 1, bias - upper, 0.0))
-    w1_out[...] = jnp.concatenate([v, jnp.broadcast_to(extra, (CHIPS, 8, CZ))], axis=1).astype(BF16)
-
-    def send_w1(k):
-        m, r, c = chip_at(k + 1)
-        return send(w1_out.at[m], w1_in.at[chip], w1_s, w1_r, k, r=r, c=c)
-
-    each(CHIPS - 1, lambda k: send_w1(k).start())
-    w1_in[chip] = w1_out[chip]
-
-    lax.fori_loop(1, 4, gr_step, 0)
+    relay_y(half, 2, 0)
+    wait_a(True)
+    lay_a(far)
+    lax.fori_loop(0, C // 8, gr_first, 0)
+    relay_y(1 - half, 5, 3)
+    wait_a(False)
+    ax.wait_send()
+    lay_a(1 - far)
+    lax.fori_loop(0, C // 8, gr_step, 0)
+    end_b()
+
+    def lay_b(q, carry):
+        part = b_in[:, pl.ds(q * 16, 16), :].astype(F32)
+        for h in range(2):
+            b_all[pl.ds((q * 2 + h) * TJ, TJ), :] = part[:, h * 8:(h + 1) * 8, :].reshape(TJ, S).astype(BF16)
+        return carry
+
+    lax.fori_loop(0, C // 2, lay_b, 0, unroll=4)
+
+    def p_step(n, carry):
+        rhs = b_all[pl.ds(n * 2048, 2048), :]
+        for m in range(8):
+            r = dot(a_all[m], rhs, NT).astype(BF16)
+            for q in range(16):
+                p[n * 16 + q, m * 256:(m + 1) * 256, :] = r[:, q * TJ:(q + 1) * TJ]
+        return carry
+
+    lax.fori_loop(0, 1, p_step, 0)
+
+    def send_r(k):
+        q, r = row_spot(k + 1)
+        return send(r_out.at[q], r_in.at[spot], r_s, r_r, k, r=r)
+
+    each(4, lambda g: rx(g).wait())
+
+    def sum_x(q):
+        r_out[q] = (r_keep[q] + r_xin[q].astype(F32)).astype(BF16)
+
+    each(8, sum_x)
+    each(7, lambda k: send_r(k).start())
+    r_in[spot] = r_out[spot]
+
+    lax.fori_loop(1, 2, p_step, 0)
+
+    def gw_step(g, carry):
+        x = jnp.concatenate(
+            [p[pl.ds(g * 16, 16), q * C:(q + 1) * C, :].reshape(16 * C, TJ) for q in range(TI)], axis=1
+        )
+        w0[g, :512, :] = dot(x, cot[...].reshape(TI * TJ, CZ))
+        return carry
+
+    lax.fori_loop(0, 2, gw_step, 0)
+    w0[0, 512:, :] = gb_ref[...]
+    w0[1, 512:, :] = gb_ref[...]
+    w0_copy = send(w0.at[1 - core], w0_in, w0_s, w0_r, 0, r=mate)
+    w0_copy.start()
+
 
     def send_l(k, c, slot):
         return send(l_out.at[c], l_in.at[slot], l_s, l_r, k, c=c)
@@ -308,18 +349,20 @@
 
     lax.fori_loop(0, 1, gl_step, 0)
 
-    def send_r(k):
-        q, r = row_spot(k + 1)
-        return send(r_out.at[q], r_in.at[spot], r_s, r_r, k, r=r)
-
-    each(4, lambda g: rx(g).wait())
-
-    def sum_x(q):
-        r_out[q] = (r_keep[q] + r_xin[q].astype(F32)).astype(BF16)
-
-    each(8, sum_x)
-    each(7, lambda k: send_r(k).start())
-    r_in[spot] = r_out[spot]
+    w0_copy.wait()
+    v = (w0[core, :512, :] + w0_in[:512, :]).reshape(CHIPS, 8, CZ)
+    bias = jnp.sum(w0[core, 512:, :] + w0_in[512:, :], axis=0, keepdims=True)
+    upper = bias.astype(BF16).astype(F32)
+    place = lax.broadcasted_iota(jnp.int32, (8, CZ), 0)
+    extra = jnp.where(place == 0, upper, jnp.where(place == 1, bias - upper, 0.0))
+    w1_out[...] = jnp.concatenate([v, jnp.broadcast_to(extra, (CHIPS, 8, CZ))], axis=1).astype(BF16)
+
+    def send_w1(k):
+        m, r, c = chip_at(k + 1)
+        return send(w1_out.at[m], w1_in.at[chip], w1_s, w1_r, k, r=r, c=c)
+
+    each(CHIPS - 1, lambda k: send_w1(k).start())
+    w1_in[chip] = w1_out[chip]
 
     lax.fori_loop(1, 3, gl_step, 0)
 
@@ -377,6 +420,8 @@
         total += r_in[q].astype(F32)
     flat[:OWN * C, :] = total
     lay_out(1, [flat[pl.ds(i, C, stride=OWN), :] for i in range(OWN)], gr_ref)
+    gr_copy = pltpu.make_async_copy(gr_ref, gr_hbm, out_sem.at[1])
+    gr_copy.start()
 
     def wait_l(k):
         to = lax.rem(z + 1 + k, 4) * 2
@@ -390,12 +435,19 @@
     for q in range(1, COLS):
         total += l_in[q].astype(F32)
     lay_out(0, [total[i * C:(i + 1) * C, :] for i in range(OWN)], gl_ref)
+    gl_copy = pltpu.make_async_copy(gl_ref, gl_hbm, out_sem.at[0])
+    gl_copy.start()
 
     each(CHIPS - 1, lambda k: send_w2(k, chip_at(-1 - k)[0]).wait())
     send(w_all.at[core], w_all.at[core], w3_s, w3_r, 0, r=mate).start()
     send(w_all.at[core], w_all.at[1 - core], w3_s, w3_r, 0, r=mate).wait()
     for c in range(C):
         gw_ref[pl.ds(c, C, stride=C), :] = w_all[c // 16, c % 16 * 4:c % 16 * 4 + 4].reshape(C, CZ)
+    gw_copy = pltpu.make_async_copy(gw_ref, gw_hbm, out_sem.at[2])
+    gw_copy.start()
+    gl_copy.wait()
+    gr_copy.wait()
+    gw_copy.wait()
     each(4, lambda q: pair_copy(q).wait())
 
 
@@ -413,9 +465,18 @@
             jax.ShapeDtypeStruct((C * C, CZ), F32),
             jax.ShapeDtypeStruct((1, CZ), F32),
         ),
-        in_specs=[vmem, vmem, vmem, vmem, hbm],
-        out_specs=(hbm, vmem, vmem, vmem, vmem),
+        in_specs=[hbm, hbm, hbm, vmem, hbm],
+        out_specs=(hbm, hbm, hbm, hbm, vmem),
         scratch_shapes=[
+            pltpu.VMEM((OWN, S * C), BF16),
+            pltpu.VMEM((OWN, S * C), BF16),
+            pltpu.VMEM((C * C, CZ), BF16),
+            pltpu.VMEM((OWN, S * C), F32),
+            pltpu.VMEM((OWN, S * C), F32),
+            pltpu.VMEM((C * C, CZ), F32),
+            pltpu.VMEM((4, S, 8 * TJ), F32),
+            dma((3,)),
+            dma((3,)),
             pltpu.VMEM((8, CZ), F32),
             pltpu.VMEM((2, own, S), F32),
             pltpu.VMEM((C * C, CZ), F32),
@@ -423,7 +484,7 @@
             pltpu.VMEM((C, TI * C, TJ), BF16),
             pltpu.VMEM((C, TI * C, TJ), BF16),
             pltpu.VMEM((COLS, own, S), BF16),
-            pltpu.VMEM((S, TI * C), BF16),
+            pltpu.VMEM((S, TI * C // 2), BF16),
             pltpu.VMEM((ROWS, own, S), BF16),
             pltpu.VMEM((C * TJ, S), BF16),
             pltpu.VMEM((C * C, CZ), BF16),
@@ -464,9 +525,16 @@
             jax.ShapeDtypeStruct((1, CZ), F32),
             jax.ShapeDtypeStruct((TI, TJ, CZ), BF16),
         ),
-        in_specs=[vmem] * 5,
+        in_specs=[hbm] * 5,
         out_specs=(hbm,) * 5,
-        scratch_shapes=[dma((5,))],
+        scratch_shapes=[
+            pltpu.VMEM((OWN, S * C), F32),
+            pltpu.VMEM((OWN, S * C), F32),
+            pltpu.VMEM((C * C, CZ), F32),
+            pltpu.VMEM((1, CZ), F32),
+            pltpu.VMEM((TI, TJ, CZ), BF16),
+            dma((2, 8)),
+        ],
         name="finish",
     )(gl, gr, gw, gb, pair)
     return pair, grad_left, grad_right, grad_weight, grad_bias.reshape(CZ)

time: 66.4 us -> 62 us (0.934)
  Pallas kernels: 65.4 us -> 61 us
    pallas_call x1, Pallas kernels: 61.9 us -> 58.2 us  [per_device(): pl.pallas_call(kernel, out_shape=(jax.ShapeDtypeStruct((TI, TJ, CZ), BF16...]
    pallas_call x1, Pallas kernels: 3.53 us -> 2.81 us  [per_device(): pl.pallas_call(finish, out_shape=(jax.ShapeDtypeStruct((OWN, S * C), F32)...]
where the time goes in v5:
time: 62 us; the launch traced here: 61.8 us
  Pallas kernels  61 us (98%)
  between operations  0.8 us (1%)
    pallas_call x1, Pallas kernels, per_device(): pl.pallas_call(kernel, out_shape=(jax.ShapeDtypeStruct((TI, TJ, CZ), BF16...  58.2 us
    pallas_call x1, Pallas kernels, per_device(): pl.pallas_call(finish, out_shape=(jax.ShapeDtypeStruct((OWN, S * C), F32)...  2.81 us

profile of v5, /device:TPU:1, one launch (start us, length us, event | category | flops | bytes accessed | tf_op | source)
XLA Modules:
  0.0 61.8 jit_solution(16995830586417521548)
XLA Ops:
  0.6 58.2 %outer_product_mean.1 = (bf16[64,128,128]{2,1,0:T(8,128)(2,1)}, f32[8,4096]{1,0:T(8,128)}, f32[8,4096]{1,0:T(8,128)}, f32[1024,128]{1,0:T(8,128)}, f32[1,128]{1,0:T(1,128)}) custom-call(bf16[8,4096]{1,0:T(8,128)(2,1)} %left_hbm.1, bf16[8,4096]{1,0:T(8,128)(2,1)} %right_hbm.1, bf16[1024,128]{1,0:T(8,128)(2,1)} %weight_hbm.1, f32[1,128]{1,0:T(1,128)} %bitcast.2, ...), custom_call_target="tpu_custom_call" | custom-call | tf_op jit(solution)/shard_map/outer_product_mean/pallas_call | solution.py:459
  58.9 2.8 %finish.1 = (f32[8,4096]{1,0:T(8,128)}, f32[8,4096]{1,0:T(8,128)}, f32[1024,128]{1,0:T(8,128)}, f32[1,128]{1,0:T(1,128)}, bf16[64,128,128]{2,1,0:T(8,128)(2,1)}) custom-call(f32[8,4096]{1,0:T(8,128)} %get-tuple-element.15.refs_0_, f32[8,4096]{1,0:T(8,128)} %get-tuple-element.16.refs_1_, f32[1024,128]{1,0:T(8,128)} %get-tuple-element.17.refs_2_, ...), custom_call_target="tpu_custom_call" | custom-call | tf_op jit(solution)/shard_map/finish/pallas_call | solution.py:519

commit v6 on v5

--- a/solution.py
+++ b/solution.py
@@ -63,10 +63,10 @@
     pair_hbm, gl_hbm, gr_hbm, gw_hbm, bsum_ref,
     left_ref, right_ref, weight_ref, gl_ref, gr_ref, gw_ref, r_acc, in_sem, out_sem,
     gb_ref, stage, flat, cot, d, p, a_all, a_t, b_in, b_all, w_ref, w_t, pair,
-    l_out, l_in, r_keep, r_x, r_xin, r_out, r_in,
+    l_out, l_in, l_x, l_xin, r_keep, r_x, r_xin, r_out, r_in,
     w0, w0_in, w1_out, w1_in, w2_out, w_all,
     cot_sem, pair_sem, ax_s, ax_r, az_s, az_r, bc_s, bc_r, bx_s, bx_r, by_s, by_r,
-    l_s, l_r, rx_s, rx_r, r_s, r_r,
+    l_s, l_r, lx_s, lx_r, rx_s, rx_r, r_s, r_r,
     w0_s, w0_r, w1_s, w1_r, w2_s, w2_r, w3_s, w3_r,
 ):
     row = lax.axis_index("row")
@@ -92,9 +92,19 @@
         q = lax.rem(spot + n + 8, 8)
         return q, q * 2 + core
 
-    def chip_at(n):
-        m = lax.rem(chip + n + CHIPS, CHIPS)
-        return m, lax.div(m, COLS) * 2 + core, lax.rem(m, COLS)
+    def chip_at(k, sign):
+        def step(v):
+            return lax.rem(2 + 3 * v - lax.div(v * (v - 1), 2), 4)
+
+        def turn(v, n):
+            return lax.rem(v + sign * step(n) + 4, 4)
+
+        x2 = turn(far * 2 + half, lax.div(k, 16))
+        y2 = turn(y, lax.rem(lax.div(k, 4), 4))
+        z2 = turn(z, lax.rem(k, 4))
+        spot2 = lax.rem(x2, 2) * 4 + y2
+        col2 = z2 * 2 + lax.div(x2, 2)
+        return spot2 * COLS + col2, spot2 * 2 + core, col2
 
     def send(src, dst, ss, rs, k, r=None, c=None):
         return pltpu.make_async_remote_copy(
@@ -131,8 +141,10 @@
     def greet(r, c):
         pl.semaphore_signal(barrier, inc=1, device_id=(r, c), device_id_type=MESH)
 
-    each(COLS - 1, lambda k: greet(row, lax.rem(col + k + 1, COLS)))
-    each(7, lambda k: greet(row_spot(k + 1)[1], col))
+    greet(near, col)
+    greet(row, other)
+    each(3, lambda k: greet(row_y(k + 1), col))
+    each(3, lambda k: greet(row, col_z(k + 1)))
     greet(mate, col)
 
     each(4, lambda q: cot_copy(q).start())
@@ -155,7 +167,7 @@
     b_in[row] = flat[:OWN * C, :].astype(BF16)
     a_ref = a_all.at[col]
     b_ref = b_in.at[row]
-    pl.semaphore_wait(barrier, 15)
+    pl.semaphore_wait(barrier, 9)
 
     bx = send(b_ref, b_in.at[row], bx_s, bx_r, 0, r=near)
     bx.start()
@@ -237,9 +249,9 @@
         gb_ref[...] += jnp.sum(block.astype(F32).reshape(group * TJ // 8, 8, CZ), axis=0)
         return carry
 
-    lax.fori_loop(0, 3, d_step, 0)
+    lax.fori_loop(0, 2, d_step, 0)
     relay_x()
-    lax.fori_loop(3, 4, d_step, 0)
+    lax.fori_loop(2, 4, d_step, 0)
     def rx(g):
         part = pl.ds(g * 64, 64)
         return send(r_x.at[:, part], r_xin.at[:, part], rx_s, rx_r, g, r=mate)
@@ -334,8 +346,9 @@
     w0_copy.start()
 
 
-    def send_l(k, c, slot):
-        return send(l_out.at[c], l_in.at[slot], l_s, l_r, k, c=c)
+    def send_l(m, slot):
+        to = lax.rem(z + 1 + m, 4)
+        return send(l_out.at[pl.ds(to * 2, 2)], l_in.at[pl.ds(slot * 2, 2)], l_s, l_r, m, c=to * 2 + far)
 
     def gl_step(m, carry):
         to = lax.rem(z + 1 + m, 4)
@@ -343,8 +356,7 @@
         r = (dot(x, b_all[...]) * (1.0 / S)).astype(BF16)
         for h in range(2):
             l_out[to * 2 + h] = r[h * 256:(h + 1) * 256, :]
-        send_l(m * 2, to * 2 + far, col).start()
-        send_l(m * 2 + 1, to * 2 + 1 - far, col).start()
+        send_l(m, z).start()
         return carry
 
     lax.fori_loop(0, 1, gl_step, 0)
@@ -358,9 +370,10 @@
     w1_out[...] = jnp.concatenate([v, jnp.broadcast_to(extra, (CHIPS, 8, CZ))], axis=1).astype(BF16)
 
     def send_w1(k):
-        m, r, c = chip_at(k + 1)
+        m, r, c = chip_at(k, 1)
         return send(w1_out.at[m], w1_in.at[chip], w1_s, w1_r, k, r=r, c=c)
 
+    each(7, lambda k: send(r_out.at[0], r_in.at[row_spot(-1 - k)[0]], r_s, r_r, k, r=near).wait())
     each(CHIPS - 1, lambda k: send_w1(k).start())
     w1_in[chip] = w1_out[chip]
 
@@ -371,8 +384,7 @@
         r = (dot(x, b_all[...]) * (1.0 / S)).astype(BF16)
         for h in range(2):
             l_out[z * 2 + h] = r[h * 256:(h + 1) * 256, :]
-        send_l(6, z * 2 + 1 - far, col).start()
-        l_in[col] = l_out[col]
+        l_in[pl.ds(z * 2, 2)] = l_out[pl.ds(z * 2, 2)]
 
     gl_last()
 
@@ -389,8 +401,8 @@
     lax.fori_loop(0, 2, pair_step, 0)
 
     def wait_w1(k):
-        m, r, c = chip_at(k + 1)
-        send(w1_out.at[m], w1_in.at[chip_at(-1 - k)[0]], w1_s, w1_r, k, r=r, c=c).wait()
+        m, r, c = chip_at(k, 1)
+        send(w1_out.at[m], w1_in.at[chip_at(k, -1)[0]], w1_s, w1_r, k, r=r, c=c).wait()
 
     each(CHIPS - 1, wait_w1)
     s1 = w1_in[0].astype(F32)
@@ -400,7 +412,7 @@
     bsum_ref[...] = s1[8:9, :] + s1[9:10, :]
 
     def send_w2(k, slot):
-        _, r, c = chip_at(k + 1)
+        _, r, c = chip_at(k, 1)
         return send(w2_out, w_all.at[core, slot], w2_s, w2_r, k, r=r, c=c)
 
     each(CHIPS - 1, lambda k: send_w2(k, chip).start())
@@ -414,7 +426,6 @@
         for q in range(C):
             out[:, q * S:(q + 1) * S] = stage[n, pl.ds(q, OWN, stride=C), :]
 
-    each(7, lambda k: send(r_out.at[0], r_in.at[row_spot(-1 - k)[0]], r_s, r_r, k, r=near).wait())
     total = r_in[0].astype(F32)
     for q in range(1, 8):
         total += r_in[q].astype(F32)
@@ -423,22 +434,25 @@
     gr_copy = pltpu.make_async_copy(gr_ref, gr_hbm, out_sem.at[1])
     gr_copy.start()
 
-    def wait_l(k):
-        to = lax.rem(z + 1 + k, 4) * 2
-        of = lax.rem(z + 3 - k, 4) * 2
-        send_l(k * 2, to + far, of + far).wait()
-        send_l(k * 2 + 1, to + 1 - far, of + 1 - far).wait()
-
-    each(3, wait_l)
-    send_l(6, other, other).wait()
-    total = l_in[0].astype(F32)
-    for q in range(1, COLS):
-        total += l_in[q].astype(F32)
+    each(3, lambda m: send_l(m, lax.rem(z + 3 - m, 4)).wait())
+    theirs = l_in[1 - far].astype(F32)
+    for q in range(1, 4):
+        theirs += l_in[2 * q + 1 - far].astype(F32)
+    l_x[...] = theirs.astype(BF16)
+    lx = send(l_x, l_xin, lx_s, lx_r, 0, c=other)
+    lx.start()
+    total = l_in[far].astype(F32)
+    for q in range(1, 4):
+        total += l_in[2 * q + far].astype(F32)
+    stage[0] = total
+
+    lx.wait()
+    total = stage[0] + l_xin[...].astype(F32)
     lay_out(0, [total[i * C:(i + 1) * C, :] for i in range(OWN)], gl_ref)
     gl_copy = pltpu.make_async_copy(gl_ref, gl_hbm, out_sem.at[0])
     gl_copy.start()
 
-    each(CHIPS - 1, lambda k: send_w2(k, chip_at(-1 - k)[0]).wait())
+    each(CHIPS - 1, lambda k: send_w2(k, chip_at(k, -1)[0]).wait())
     send(w_all.at[core], w_all.at[core], w3_s, w3_r, 0, r=mate).start()
     send(w_all.at[core], w_all.at[1 - core], w3_s, w3_r, 0, r=mate).wait()
     for c in range(C):
@@ -492,6 +506,8 @@
             pltpu.VMEM((TI, TJ, CZ), BF16),
             pltpu.VMEM((COLS, own, S), BF16),
             pltpu.VMEM((COLS, own, S), BF16),
+            pltpu.VMEM((own, S), BF16),
+            pltpu.VMEM((own, S), BF16),
             pltpu.VMEM((8, own, S), F32),
             pltpu.VMEM((8, own, S), BF16),
             pltpu.VMEM((8, own, S), BF16),
@@ -506,7 +522,7 @@
             dma((4,)), dma((4,)),
             dma((1,)), dma((1,)), dma((6,)), dma((6,)),
             dma((8,)), dma((8,)), dma((1,)), dma((1,)), dma((6,)), dma((6,)),
-            dma((7,)), dma((7,)),
+            dma((3,)), dma((3,)), dma((1,)), dma((1,)),
             dma((4,)), dma((4,)), dma((7,)), dma((7,)),
             dma((1,)), dma((1,)), dma((CHIPS - 1,)), dma((CHIPS - 1,)),
             dma((CHIPS - 1,)), dma((CHIPS - 1,)), dma((1,)), dma((1,)),

time: 62 us -> 60.7 us (0.979)
  Pallas kernels: 61 us -> 59.1 us
    pallas_call x1, Pallas kernels: 58.2 us -> 56.3 us  [per_device(): pl.pallas_call(kernel, out_shape=(jax.ShapeDtypeStruct((TI, TJ, CZ), BF16...]
where the time goes in v6:
time: 60.7 us; the launch traced here: 59.9 us
  Pallas kernels  59.1 us (97%)
  between operations  0.8 us (1%)
    pallas_call x1, Pallas kernels, per_device(): pl.pallas_call(kernel, out_shape=(jax.ShapeDtypeStruct((TI, TJ, CZ), BF16...  56.3 us
    pallas_call x1, Pallas kernels, per_device(): pl.pallas_call(finish, out_shape=(jax.ShapeDtypeStruct((OWN, S * C), F32)...  2.81 us

profile of v6, /device:TPU:1, one launch (start us, length us, event | category | flops | bytes accessed | tf_op | source)
XLA Modules:
  0.0 59.9 jit_solution(11210535003053903939)
XLA Ops:
  0.6 56.3 %outer_product_mean.1 = (bf16[64,128,128]{2,1,0:T(8,128)(2,1)}, f32[8,4096]{1,0:T(8,128)}, f32[8,4096]{1,0:T(8,128)}, f32[1024,128]{1,0:T(8,128)}, f32[1,128]{1,0:T(1,128)}) custom-call(bf16[8,4096]{1,0:T(8,128)(2,1)} %left_hbm.1, bf16[8,4096]{1,0:T(8,128)(2,1)} %right_hbm.1, bf16[1024,128]{1,0:T(8,128)(2,1)} %weight_hbm.1, f32[1,128]{1,0:T(1,128)} %bitcast.2, ...), custom_call_target="tpu_custom_call" | custom-call | tf_op jit(solution)/shard_map/outer_product_mean/pallas_call | solution.py:473
  57.0 2.8 %finish.1 = (f32[8,4096]{1,0:T(8,128)}, f32[8,4096]{1,0:T(8,128)}, f32[1024,128]{1,0:T(8,128)}, f32[1,128]{1,0:T(1,128)}, bf16[64,128,128]{2,1,0:T(8,128)(2,1)}) custom-call(f32[8,4096]{1,0:T(8,128)} %get-tuple-element.15.refs_0_, f32[8,4096]{1,0:T(8,128)} %get-tuple-element.16.refs_1_, f32[1024,128]{1,0:T(8,128)} %get-tuple-element.17.refs_2_, ...), custom_call_target="tpu_custom_call" | custom-call | tf_op jit(solution)/shard_map/finish/pallas_call | solution.py:535

commit v7 on v6

--- a/solution.py
+++ b/solution.py
@@ -21,6 +21,12 @@
 NT = (((1,), (1,)), ((), ()))
 F32 = jnp.float32
 BF16 = jnp.bfloat16
+
+
+STEPS = sorted(
+    ((n // 16, n // 4 % 4, n % 4) for n in range(1, CHIPS)),
+    key=lambda t: (-sum(min(v, 4 - v) for v in t), t),
+)
 
 
 def dot(a, b, dims=NN):
@@ -92,19 +98,16 @@
         q = lax.rem(spot + n + 8, 8)
         return q, q * 2 + core
 
-    def chip_at(k, sign):
-        def step(v):
-            return lax.rem(2 + 3 * v - lax.div(v * (v - 1), 2), 4)
-
-        def turn(v, n):
-            return lax.rem(v + sign * step(n) + 4, 4)
-
-        x2 = turn(far * 2 + half, lax.div(k, 16))
-        y2 = turn(y, lax.rem(lax.div(k, 4), 4))
-        z2 = turn(z, lax.rem(k, 4))
-        spot2 = lax.rem(x2, 2) * 4 + y2
-        col2 = z2 * 2 + lax.div(x2, 2)
-        return spot2 * COLS + col2, spot2 * 2 + core, col2
+    x = far * 2 + half
+    xs, ys, zs = ([lax.rem(v + n, 4) for n in range(4)] for v in (x, y, z))
+    row_x = [lax.rem(v, 2) * 8 + core for v in xs]
+    col_x = [lax.div(v, 2) for v in xs]
+
+    def chip_at(k):
+        dx, dy, dz = STEPS[k]
+        r = row_x[dx] + ys[dy] * 2
+        c = col_x[dx] + zs[dz] * 2
+        return lax.div(r, 2) * COLS + c, r, c
 
     def send(src, dst, ss, rs, k, r=None, c=None):
         return pltpu.make_async_remote_copy(
@@ -308,11 +311,11 @@
     lax.fori_loop(0, C // 2, lay_b, 0, unroll=4)
 
     def p_step(n, carry):
-        rhs = b_all[pl.ds(n * 2048, 2048), :]
+        rhs = b_all[pl.ds(n * 1024, 1024), :]
         for m in range(8):
             r = dot(a_all[m], rhs, NT).astype(BF16)
-            for q in range(16):
-                p[n * 16 + q, m * 256:(m + 1) * 256, :] = r[:, q * TJ:(q + 1) * TJ]
+            for q in range(8):
+                p[n * 8 + q, m * 256:(m + 1) * 256, :] = r[:, q * TJ:(q + 1) * TJ]
         return carry
 
     lax.fori_loop(0, 1, p_step, 0)
@@ -330,20 +333,23 @@
     each(7, lambda k: send_r(k).start())
     r_in[spot] = r_out[spot]
 
-    lax.fori_loop(1, 2, p_step, 0)
-
-    def gw_step(g, carry):
+    lax.fori_loop(1, 4, p_step, 0)
+
+    w0[0, 512:, :] = gb_ref[...]
+    w0[1, 512:, :] = gb_ref[...]
+    w0_copy = send(w0.at[1 - core], w0_in, w0_s, w0_r, 0, r=mate)
+
+    def gw_step(n, carry):
+        g = lax.rem(n + 1 + core, 2)
         x = jnp.concatenate(
             [p[pl.ds(g * 16, 16), q * C:(q + 1) * C, :].reshape(16 * C, TJ) for q in range(TI)], axis=1
         )
         w0[g, :512, :] = dot(x, cot[...].reshape(TI * TJ, CZ))
         return carry
 
-    lax.fori_loop(0, 2, gw_step, 0)
-    w0[0, 512:, :] = gb_ref[...]
-    w0[1, 512:, :] = gb_ref[...]
-    w0_copy = send(w0.at[1 - core], w0_in, w0_s, w0_r, 0, r=mate)
+    lax.fori_loop(0, 1, gw_step, 0)
     w0_copy.start()
+    lax.fori_loop(1, 2, gw_step, 0)
 
 
     def send_l(m, slot):
@@ -359,8 +365,6 @@
         send_l(m, z).start()
         return carry
 
-    lax.fori_loop(0, 1, gl_step, 0)
-
     w0_copy.wait()
     v = (w0[core, :512, :] + w0_in[:512, :]).reshape(CHIPS, 8, CZ)
     bias = jnp.sum(w0[core, 512:, :] + w0_in[512:, :], axis=0, keepdims=True)
@@ -370,14 +374,15 @@
     w1_out[...] = jnp.concatenate([v, jnp.broadcast_to(extra, (CHIPS, 8, CZ))], axis=1).astype(BF16)
 
     def send_w1(k):
-        m, r, c = chip_at(k, 1)
+        m, r, c = chip_at(k)
         return send(w1_out.at[m], w1_in.at[chip], w1_s, w1_r, k, r=r, c=c)
 
     each(7, lambda k: send(r_out.at[0], r_in.at[row_spot(-1 - k)[0]], r_s, r_r, k, r=near).wait())
-    each(CHIPS - 1, lambda k: send_w1(k).start())
+    for k in range(CHIPS - 1):
+        send_w1(k).start()
     w1_in[chip] = w1_out[chip]
 
-    lax.fori_loop(1, 3, gl_step, 0)
+    lax.fori_loop(0, 3, gl_step, 0)
 
     def gl_last():
         x = jnp.concatenate([d[q, pl.ds(z * 512, 512), :] for q in range(C)], axis=1)
@@ -401,8 +406,7 @@
     lax.fori_loop(0, 2, pair_step, 0)
 
     def wait_w1(k):
-        m, r, c = chip_at(k, 1)
-        send(w1_out.at[m], w1_in.at[chip_at(k, -1)[0]], w1_s, w1_r, k, r=r, c=c).wait()
+        send(w1_out.at[k], w1_in.at[k], w1_s, w1_r, k, r=near).wait()
 
     each(CHIPS - 1, wait_w1)
     s1 = w1_in[0].astype(F32)
@@ -411,11 +415,12 @@
     w2_out[...] = s1[:8, :]
     bsum_ref[...] = s1[8:9, :] + s1[9:10, :]
 
-    def send_w2(k, slot):
-        _, r, c = chip_at(k, 1)
-        return send(w2_out, w_all.at[core, slot], w2_s, w2_r, k, r=r, c=c)
-
-    each(CHIPS - 1, lambda k: send_w2(k, chip).start())
+    def send_w2(k):
+        _, r, c = chip_at(k)
+        return send(w2_out, w_all.at[core, chip], w2_s, w2_r, k, r=r, c=c)
+
+    for k in range(CHIPS - 1):
+        send_w2(k).start()
     w_all[core, chip] = w2_out[...]
 
     lax.fori_loop(2, 4, pair_step, 0)
@@ -452,7 +457,7 @@
     gl_copy = pltpu.make_async_copy(gl_ref, gl_hbm, out_sem.at[0])
     gl_copy.start()
 
-    each(CHIPS - 1, lambda k: send_w2(k, chip_at(k, -1)[0]).wait())
+    each(CHIPS - 1, lambda k: send(w2_out, w_all.at[core, k], w2_s, w2_r, k, r=near).wait())
     send(w_all.at[core], w_all.at[core], w3_s, w3_r, 0, r=mate).start()
     send(w_all.at[core], w_all.at[1 - core], w3_s, w3_r, 0, r=mate).wait()
     for c in range(C):

time: 60.7 us -> 63.4 us (1.044)
  Pallas kernels: 59.1 us -> 62.4 us
    pallas_call x1, Pallas kernels: 56.3 us -> 59.6 us  [per_device(): pl.pallas_call(kernel, out_shape=(jax.ShapeDtypeStruct((TI, TJ, CZ), BF16...]
where the time goes in v7:
time: 63.4 us; the launch traced here: 63.2 us
  Pallas kernels  62.4 us (98%)
  between operations  0.8 us (1%)
    pallas_call x1, Pallas kernels, per_device(): pl.pallas_call(kernel, out_shape=(jax.ShapeDtypeStruct((TI, TJ, CZ), BF16...  59.6 us
    pallas_call x1, Pallas kernels, per_device(): pl.pallas_call(finish, out_shape=(jax.ShapeDtypeStruct((OWN, S * C), F32)...  2.81 us

profile of v7, /device:TPU:1, one launch (start us, length us, event | category | flops | bytes accessed | tf_op | source)
XLA Modules:
  0.0 63.2 jit_solution(10378681358027372927)
XLA Ops:
  0.6 59.6 %outer_product_mean.1 = (bf16[64,128,128]{2,1,0:T(8,128)(2,1)}, f32[8,4096]{1,0:T(8,128)}, f32[8,4096]{1,0:T(8,128)}, f32[1024,128]{1,0:T(8,128)}, f32[1,128]{1,0:T(1,128)}) custom-call(bf16[8,4096]{1,0:T(8,128)(2,1)} %left_hbm.1, bf16[8,4096]{1,0:T(8,128)(2,1)} %right_hbm.1, bf16[1024,128]{1,0:T(8,128)(2,1)} %weight_hbm.1, f32[1,128]{1,0:T(1,128)} %bitcast.2, ...), custom_call_target="tpu_custom_call" | custom-call | tf_op jit(solution)/shard_map/outer_product_mean/pallas_call | solution.py:478
  60.2 2.8 %finish.1 = (f32[8,4096]{1,0:T(8,128)}, f32[8,4096]{1,0:T(8,128)}, f32[1024,128]{1,0:T(8,128)}, f32[1,128]{1,0:T(1,128)}, bf16[64,128,128]{2,1,0:T(8,128)(2,1)}) custom-call(f32[8,4096]{1,0:T(8,128)} %get-tuple-element.15.refs_0_, f32[8,4096]{1,0:T(8,128)} %get-tuple-element.16.refs_1_, f32[1024,128]{1,0:T(8,128)} %get-tuple-element.17.refs_2_, ...), custom_call_target="tpu_custom_call" | custom-call | tf_op jit(solution)/shard_map/finish/pallas_call | solution.py:540

commit v8 on v7

--- a/solution.py
+++ b/solution.py
@@ -25,7 +25,7 @@
 
 STEPS = sorted(
     ((n // 16, n // 4 % 4, n % 4) for n in range(1, CHIPS)),
-    key=lambda t: (-sum(min(v, 4 - v) for v in t), t),
+    key=lambda t: tuple((2, 1, 3, 0).index(v) for v in t),
 )
 
 
@@ -311,11 +311,11 @@
     lax.fori_loop(0, C // 2, lay_b, 0, unroll=4)
 
     def p_step(n, carry):
-        rhs = b_all[pl.ds(n * 1024, 1024), :]
+        rhs = b_all[pl.ds(n * 2048, 2048), :]
         for m in range(8):
             r = dot(a_all[m], rhs, NT).astype(BF16)
-            for q in range(8):
-                p[n * 8 + q, m * 256:(m + 1) * 256, :] = r[:, q * TJ:(q + 1) * TJ]
+            for q in range(16):
+                p[n * 16 + q, m * 256:(m + 1) * 256, :] = r[:, q * TJ:(q + 1) * TJ]
         return carry
 
     lax.fori_loop(0, 1, p_step, 0)
@@ -333,23 +333,20 @@
     each(7, lambda k: send_r(k).start())
     r_in[spot] = r_out[spot]
 
-    lax.fori_loop(1, 4, p_step, 0)
-
-    w0[0, 512:, :] = gb_ref[...]
-    w0[1, 512:, :] = gb_ref[...]
-    w0_copy = send(w0.at[1 - core], w0_in, w0_s, w0_r, 0, r=mate)
-
-    def gw_step(n, carry):
-        g = lax.rem(n + 1 + core, 2)
+    lax.fori_loop(1, 2, p_step, 0)
+
+    def gw_step(g, carry):
         x = jnp.concatenate(
             [p[pl.ds(g * 16, 16), q * C:(q + 1) * C, :].reshape(16 * C, TJ) for q in range(TI)], axis=1
         )
         w0[g, :512, :] = dot(x, cot[...].reshape(TI * TJ, CZ))
         return carry
 
-    lax.fori_loop(0, 1, gw_step, 0)
+    lax.fori_loop(0, 2, gw_step, 0)
+    w0[0, 512:, :] = gb_ref[...]
+    w0[1, 512:, :] = gb_ref[...]
+    w0_copy = send(w0.at[1 - core], w0_in, w0_s, w0_r, 0, r=mate)
     w0_copy.start()
-    lax.fori_loop(1, 2, gw_step, 0)
 
 
     def send_l(m, slot):
@@ -365,6 +362,8 @@
         send_l(m, z).start()
         return carry
 
+    lax.fori_loop(0, 1, gl_step, 0)
+
     w0_copy.wait()
     v = (w0[core, :512, :] + w0_in[:512, :]).reshape(CHIPS, 8, CZ)
     bias = jnp.sum(w0[core, 512:, :] + w0_in[512:, :], axis=0, keepdims=True)
@@ -382,7 +381,7 @@
         send_w1(k).start()
     w1_in[chip] = w1_out[chip]
 
-    lax.fori_loop(0, 3, gl_step, 0)
+    lax.fori_loop(1, 3, gl_step, 0)
 
     def gl_last():
         x = jnp.concatenate([d[q, pl.ds(z * 512, 512), :] for q in range(C)], axis=1)
@@ -403,7 +402,7 @@
         pair_copy(g).start()
         return carry
 
-    lax.fori_loop(0, 2, pair_step, 0)
+    lax.fori_loop(0, 1, pair_step, 0)
 
     def wait_w1(k):
         send(w1_out.at[k], w1_in.at[k], w1_s, w1_r, k, r=near).wait()
@@ -423,7 +422,7 @@
         send_w2(k).start()
     w_all[core, chip] = w2_out[...]
 
-    lax.fori_loop(2, 4, pair_step, 0)
+    lax.fori_loop(1, 4, pair_step, 0)
 
     def lay_out(n, rows, out):
         for g in range(2):

time: 63.4 us -> 60.6 us (0.956)
  Pallas kernels: 62.4 us -> 59.6 us
    pallas_call x1, Pallas kernels: 59.6 us -> 56.8 us  [per_device(): pl.pallas_call(kernel, out_shape=(jax.ShapeDtypeStruct((TI, TJ, CZ), BF16...]
where the time goes in v8:
time: 60.6 us; the launch traced here: 60.4 us
  Pallas kernels  59.6 us (98%)
  between operations  0.8 us (1%)
    pallas_call x1, Pallas kernels, per_device(): pl.pallas_call(kernel, out_shape=(jax.ShapeDtypeStruct((TI, TJ, CZ), BF16...  56.8 us
    pallas_call x1, Pallas kernels, per_device(): pl.pallas_call(finish, out_shape=(jax.ShapeDtypeStruct((OWN, S * C), F32)...  2.81 us

profile of v8, /device:TPU:1, one launch (start us, length us, event | category | flops | bytes accessed | tf_op | source)
XLA Modules:
  0.0 60.4 jit_solution(8020226631632299003)
XLA Ops:
  0.6 56.8 %outer_product_mean.1 = (bf16[64,128,128]{2,1,0:T(8,128)(2,1)}, f32[8,4096]{1,0:T(8,128)}, f32[8,4096]{1,0:T(8,128)}, f32[1024,128]{1,0:T(8,128)}, f32[1,128]{1,0:T(1,128)}) custom-call(bf16[8,4096]{1,0:T(8,128)(2,1)} %left_hbm.1, bf16[8,4096]{1,0:T(8,128)(2,1)} %right_hbm.1, bf16[1024,128]{1,0:T(8,128)(2,1)} %weight_hbm.1, f32[1,128]{1,0:T(1,128)} %bitcast.2, ...), custom_call_target="tpu_custom_call" | custom-call | tf_op jit(solution)/shard_map/outer_product_mean/pallas_call | solution.py:477
  57.4 2.8 %finish.1 = (f32[8,4096]{1,0:T(8,128)}, f32[8,4096]{1,0:T(8,128)}, f32[1024,128]{1,0:T(8,128)}, f32[1,128]{1,0:T(1,128)}, bf16[64,128,128]{2,1,0:T(8,128)(2,1)}) custom-call(f32[8,4096]{1,0:T(8,128)} %get-tuple-element.15.refs_0_, f32[8,4096]{1,0:T(8,128)} %get-tuple-element.16.refs_1_, f32[1024,128]{1,0:T(8,128)} %get-tuple-element.17.refs_2_, ...), custom_call_target="tpu_custom_call" | custom-call | tf_op jit(solution)/shard_map/finish/pallas_call | solution.py:539

commit v9 on v8

--- a/solution.py
+++ b/solution.py
@@ -362,7 +362,7 @@
         send_l(m, z).start()
         return carry
 
-    lax.fori_loop(0, 1, gl_step, 0)
+    lax.fori_loop(0, 2, gl_step, 0)
 
     w0_copy.wait()
     v = (w0[core, :512, :] + w0_in[:512, :]).reshape(CHIPS, 8, CZ)
@@ -381,7 +381,7 @@
         send_w1(k).start()
     w1_in[chip] = w1_out[chip]
 
-    lax.fori_loop(1, 3, gl_step, 0)
+    lax.fori_loop(2, 3, gl_step, 0)
 
     def gl_last():
         x = jnp.concatenate([d[q, pl.ds(z * 512, 512), :] for q in range(C)], axis=1)

time: 60.6 us -> 60.4 us (level)
  no operation moved by 1% of the time
where the time goes in v9:
time: 60.4 us; the launch traced here: 60.2 us
  Pallas kernels  59.4 us (98%)
  between operations  0.8 us (1%)
    pallas_call x1, Pallas kernels, per_device(): pl.pallas_call(kernel, out_shape=(jax.ShapeDtypeStruct((TI, TJ, CZ), BF16...  56.6 us
    pallas_call x1, Pallas kernels, per_device(): pl.pallas_call(finish, out_shape=(jax.ShapeDtypeStruct((OWN, S * C), F32)...  2.81 us

profile of v9, /device:TPU:1, one launch (start us, length us, event | category | flops | bytes accessed | tf_op | source)
XLA Modules:
  0.0 60.2 jit_solution(14658717207179716673)
XLA Ops:
  0.6 56.6 %outer_product_mean.1 = (bf16[64,128,128]{2,1,0:T(8,128)(2,1)}, f32[8,4096]{1,0:T(8,128)}, f32[8,4096]{1,0:T(8,128)}, f32[1024,128]{1,0:T(8,128)}, f32[1,128]{1,0:T(1,128)}) custom-call(bf16[8,4096]{1,0:T(8,128)(2,1)} %left_hbm.1, bf16[8,4096]{1,0:T(8,128)(2,1)} %right_hbm.1, bf16[1024,128]{1,0:T(8,128)(2,1)} %weight_hbm.1, f32[1,128]{1,0:T(1,128)} %bitcast.2, ...), custom_call_target="tpu_custom_call" | custom-call | tf_op jit(solution)/shard_map/outer_product_mean/pallas_call | solution.py:477
  57.2 2.8 %finish.1 = (f32[8,4096]{1,0:T(8,128)}, f32[8,4096]{1,0:T(8,128)}, f32[1024,128]{1,0:T(8,128)}, f32[1,128]{1,0:T(1,128)}, bf16[64,128,128]{2,1,0:T(8,128)(2,1)}) custom-call(f32[8,4096]{1,0:T(8,128)} %get-tuple-element.15.refs_0_, f32[8,4096]{1,0:T(8,128)} %get-tuple-element.16.refs_1_, f32[1024,128]{1,0:T(8,128)} %get-tuple-element.17.refs_2_, ...), custom_call_target="tpu_custom_call" | custom-call | tf_op jit(solution)/shard_map/finish/pallas_call | solution.py:539
